TPU v7x, 128 devices: a whole 4x4x4 slice. The times are simulated.
128 devices in a mesh: dp: 4 (over y), slab: 32 (over x, z, core).
Axes of the slice: x: 4, y: 4, z: 4, core: 2. Of those that a mesh axis runs over, the one named last changes fastest.
Arguments:
- volume: bfloat16 [4, 64, 16, 32, 256], P('dp', 'slab'), may hold values from -6 to 6
- pre_act: bfloat16 [4, 64, 16, 32, 256], P('dp', 'slab'), may hold values from -6 to 6
- cotangent: bfloat16 [4, 64, 16, 32, 256], P('dp', 'slab'), may hold values from -0.29882812 to 0.29882812
- kernel_second: bfloat16 [27, 256, 256], replicated, may hold values from -0.078125 to 0.078125
- q_start: float32 [2, 256, 32], replicated, may hold values from -6 to 6
- error: bfloat16 [4, 32, 2, 6912, 256], P('dp', 'slab'), may hold values from -3 to 3
Outputs:
- summed_gradient: float32 [2, 6912, 256], P(None, 'slab')
- new_error: bfloat16 [4, 32, 2, 6912, 256], P('dp', 'slab')
All inputs are finite; a program needn't handle non-finite values.
Results may differ from a plain program's by a relative error of at most 0.0036.
Values may be sent and summed in bfloat16 or wider, within the bound.
A program may use at most 128 MiB of HBM per device.

v0:
```python
import jax
import jax.numpy as jnp
from jax import lax
from jax.sharding import PartitionSpec as P


def padded_2(array, sides, width):
    for axis, dim in sides:
        size, length = (lax.axis_size(axis), array.shape[dim])
        up = [(i, (i + 1) % size) for i in range(size - 1)]
        down = [(j, i) for i, j in up]
        last = lax.slice_in_dim(array, length - width, length, axis=dim)
        initial = lax.slice_in_dim(array, 0, width, axis=dim)
        before = lax.ppermute(last, axis, up)
        after = lax.ppermute(initial, axis, down)
        array = jnp.concatenate([before, array, after], axis=dim)
    return array


def tap_rows(padded, start_a, start_b, start_c, depth, height, width):
    piece = padded[start_a : start_a + depth, start_b : start_b + height, start_c : start_c + width]
    return piece.reshape(depth * height * width, piece.shape[-1])


def local_grads(padded, out_rows, depth, height, width):
    terms = []
    for k in range(27):
        piece = tap_rows(padded, k // 9, k // 3 % 3, k % 3, depth, height, width)
        terms.append(jnp.einsum("nc,nd->cd", piece, out_rows, preferred_element_type=jnp.float32))
    stacked = jnp.stack(terms)
    return stacked.reshape(27 * stacked.shape[1], stacked.shape[2])


def orthonormal(p_sum):
    highest = lax.Precision.HIGHEST
    gram = jnp.einsum("rq,rs->qs", p_sum, p_sum, precision=highest)
    lower = jnp.linalg.cholesky(gram)
    return lax.linalg.triangular_solve(lower, p_sum, left_side=False, lower=True, transpose_a=True)


def left_terms(matrix, q_one):
    return jnp.einsum("rc,cq->rq", matrix, q_one, precision=lax.Precision.HIGHEST)


def right_terms(matrix, p_hat):
    return jnp.einsum("rc,rq->cq", matrix, p_hat, precision=lax.Precision.HIGHEST)


def compress(matrix, q_one):
    p_sum = lax.psum(left_terms(matrix, q_one), ("dp", "slab"))
    p_hat = orthonormal(p_sum)
    q_sum = lax.psum(right_terms(matrix, p_hat), ("dp", "slab"))
    return (p_hat, q_sum)


def per_device(volume, pre_act, cotangent, kernel_second, q_start, error):
    depth, height, width, chans = (
        volume.shape[1],
        volume.shape[2],
        volume.shape[3],
        volume.shape[4],
    )
    stacked = jnp.stack([volume[0], pre_act[0], cotangent[0]])
    planes = padded_2(stacked, (("slab", 1),), 1)
    planes = jnp.pad(planes, ((0, 0), (0, 0), (1, 1), (1, 1), (0, 0)))
    input_pad = planes[0]
    act_pad = jnp.maximum(planes[1], jnp.zeros_like(planes[1]))
    cot_pad = planes[2]
    cot_rows = cotangent[0].reshape(depth * height * width, chans)
    error_first = error[0, 0, 0].astype(jnp.float32)
    error_second = error[0, 0, 1].astype(jnp.float32)
    matrix_second = local_grads(act_pad, cot_rows, depth, height, width) + error_second
    hat_second, qsum_second = compress(matrix_second, q_start[1])
    back = jnp.zeros((depth * height * width, chans), jnp.float32)
    for k in range(27):
        piece = tap_rows(cot_pad, 2 - k // 9, 2 - k // 3 % 3, 2 - k % 3, depth, height, width)
        back = back + jnp.einsum(
            "nd,cd->nc", piece, kernel_second[k], preferred_element_type=jnp.float32
        )
    back = back.reshape(depth, height, width, chans)
    gate = jnp.where(pre_act[0] > 0, back, jnp.zeros_like(back)).astype(jnp.bfloat16)
    gate_rows = gate.reshape(depth * height * width, chans)
    matrix_first = local_grads(input_pad, gate_rows, depth, height, width) + error_first
    hat_first, qsum_first = compress(matrix_first, q_start[0])
    highest = lax.Precision.HIGHEST
    summed_first = jnp.einsum("rq,cq->rc", hat_first, qsum_first, precision=highest)
    summed_second = jnp.einsum("rq,cq->rc", hat_second, qsum_second, precision=highest)
    devices = lax.axis_size("dp") * lax.axis_size("slab")
    new_first = (matrix_first - summed_first / devices).astype(jnp.bfloat16)
    new_second = (matrix_second - summed_second / devices).astype(jnp.bfloat16)
    new_error = jnp.stack([new_first, new_second])[None, None]
    row_count = summed_first.shape[0] // lax.axis_size("slab")
    row_start = lax.axis_index("slab") * row_count
    summed = jnp.stack([summed_first, summed_second])
    summed_share = lax.dynamic_slice_in_dim(summed, row_start, row_count, 1)
    return (summed_share, new_error)


def solution(mesh):
    in_specs = (
        P("dp", "slab", None, None, None),
        P("dp", "slab", None, None, None),
        P("dp", "slab", None, None, None),
        P(),
        P(),
        P("dp", "slab", None, None, None),
    )
    out_specs = (P(None, "slab", None), P("dp", "slab", None, None, None))
    return jax.shard_map(
        per_device, mesh=mesh, in_specs=in_specs, out_specs=out_specs, check_vma=False
    )
```

profile of v0, /device:TPU:1, one launch (start us, length us, event | category | flops | bytes accessed | tf_op | source)
XLA Modules:
  0.0 483.4 jit_solution(4283728591636989588)
XLA Ops:
  10.7 4.9 %collective-permute-start = (bf16[3,1,16,32,256]{4,3,2,1,0:T(8,128)(2,1)S(1)}, bf16[3,1,16,32,256]{4,3,2,1,0:T(8,128)(2,1)S(1)}, u32[]{:S(2)}, u32[]{:S(2)}) collective-permute-start(bf16[3,1,16,32,256]{4,3,2,1,0:T(8,128)(2,1)S(1)} %get-tuple-element.15), channel_id=1, source_target_pairs={{0,1},{1,2},{2,3},{3,4},{4,5},{5,6},{6,7},{7,8},{8,9},{9,10},{10,1... | collective-permute-start | bytes 2359304 | tf_op jit(solution)/shard_map/ppermute | solution.py:14
  15.6 1.9 collective-permute-start.1
  17.5 7.1 %slice_convert_fusion = (f32[1,1,1,6912,256]{4,3,2,1,0:T(8,128)}, f32[1,1,1,6912,256]{4,3,2,1,0:T(8,128)S(1)}) fusion(bf16[1,1,2,6912,256]{4,3,2,1,0:T(8,128)(2,1)} %param.14), kind=kLoop, calls=%fused_computation.23 | loop fusion | flops 3538944 | bytes 21233664 | tf_op jit(solution)/shard_map/convert_element_type | solution.py:71
  24.6 4.3 collective-permute-done.1
  28.9 2.1 select_maximum_fusion
  31.3 3.6 fusion.159
  34.9 3.2 fusion.160
  38.1 2.7 fusion.161
  60.1 2.9 copy-done.1
  72.8 2.8 copy-done
  75.6 6.1 %add.156 = f32[27,256,256]{2,1,0:T(8,128)S(1)} add(f32[27,256,256]{2,1,0:T(8,128)} %copy-done, f32[27,256,256]{2,1,0:T(8,128)} %bitcast.648) | non-fusion elementwise | flops 1769472 | bytes 21233664 | tf_op jit(solution)/shard_map/add | solution.py:72
  81.7 7.7 %fusion.146 = f32[6912,32]{0,1:T(8,128)} fusion(f32[6912,256]{1,0:T(8,128)S(1)} %bitcast.645, f32[2,256,32]{1,2,0:T(8,128)S(1)} %copy-done.21), kind=kOutput, calls=%fused_computation.250 | convolution fusion | flops 679477248 | bytes 7995392 | tf_op jit(solution)/shard_map/rc,cq->rq/dot_general | solution.py:42
  89.4 3.9 add.153
  93.3 7.5 %fusion.148 = f32[6912,32]{0,1:T(8,128)} fusion(f32[6912,256]{1,0:T(8,128)S(1)} %bitcast.646, f32[2,256,32]{1,2,0:T(8,128)S(1)} %copy-done.21), kind=kOutput, calls=%fused_computation.252 | convolution fusion | flops 679477248 | bytes 7995392 | tf_op jit(solution)/shard_map/rc,cq->rq/dot_general | solution.py:42
  100.9 13.8 %bitcast_add_fusion = (f32[6912,256]{1,0:T(8,128)}, f32[6912,256]{1,0:T(8,128)}) fusion(f32[27,256,256]{2,1,0:T(8,128)} %copy-done, bf16[1,1,2,6912,256]{4,3,2,1,0:T(8,128)(2,1)} %param.14, f32[27,256,256]{2,1,0:T(8,128)} %copy-done.1), kind=kLoop, calls=%fused_computation.12 | loop fusion | flops 7077888 | bytes 35389440 | tf_op jit(solution)/shard_map/add | solution.py:72
  114.7 138.2 %all-reduce.8.cloned.1.call-done = (f32[6912,32]{0,1:T(8,128)}, f32[6912,32]{0,1:T(8,128)}) async-done(((f32[6912,32]{0,1:T(8,128)}, f32[6912,32]{0,1:T(8,128)}), (f32[6912,32]{0,1:T(8,128)}, f32[6912,32]{0,1:T(8,128)})) %all-reduce.8.cloned.1.call-update) | async-done | bytes 1769488 | tf_op jit(solution)/shard_map/psum | solution.py:50
  252.8 2.3 fusion.166
  255.2 2.9 cholesky.55
  259.5 2.4 custom-call.7
  261.9 3.0 convolution_bitcast_fusion
  264.9 2.3 fusion.163
  267.3 2.9 cholesky.44
  271.6 2.4 custom-call.6
  274.0 2.1 convolution_bitcast_fusion.1
  276.1 14.7 %fusion.167 = f32[256,32]{1,0:T(8,128)} fusion(f32[6912,256]{1,0:T(8,128)} %get-tuple-element.8, f32[6912,32]{0,1:T(8,128)} %convolution_bitcast_fusion), kind=kOutput, calls=%fused_computation.281 | convolution fusion | flops 679477248 | bytes 7995392 | tf_op jit(solution)/shard_map/rc,rq->cq/dot_general | solution.py:46
  290.9 11.8 %fusion.164 = f32[256,32]{1,0:T(8,128)} fusion(f32[6912,256]{1,0:T(8,128)S(1)} %bitcast.644, f32[6912,32]{0,1:T(8,128)S(1)} %convolution_bitcast_fusion.1), kind=kOutput, calls=%fused_computation.278 | convolution fusion | flops 679477248 | bytes 7995392 | tf_op jit(solution)/shard_map/rc,rq->cq/dot_general | solution.py:46
  302.7 140.5 %all-reduce.6.cloned.1.call-done = (f32[256,32]{1,0:T(8,128)}, f32[256,32]{1,0:T(8,128)}) async-done(((f32[256,32]{1,0:T(8,128)}, f32[256,32]{1,0:T(8,128)}), (f32[256,32]{1,0:T(8,128)}, f32[256,32]{1,0:T(8,128)})) %all-reduce.6.cloned.1.call-update) | async-done | bytes 65552 | tf_op jit(solution)/shard_map/psum | solution.py:52
  443.1 7.1 %fusion.165 = f32[6912,256]{1,0:T(8,128)S(1)} fusion(f32[6912,32]{0,1:T(8,128)} %copy-done.2, f32[256,32]{1,0:T(8,128)} %get-tuple-element.4), kind=kOutput, calls=%fused_computation.279 | convolution fusion | flops 679477248 | bytes 7995392 | tf_op jit(solution)/shard_map/rq,cq->rc/dot_general | solution.py:86
  450.2 5.8 %fusion.6 = bf16[1,6912,256]{2,1,0:T(8,128)(2,1)} fusion(f32[6912,256]{1,0:T(8,128)} %get-tuple-element.9, f32[6912,256]{1,0:T(8,128)S(1)} %fusion.165), kind=kLoop, calls=%fused_computation.21 | loop fusion | flops 5308416 | bytes 17694720 | tf_op jit(solution)/shard_map/stack | solution.py:91
  456.1 6.9 %fusion.168 = f32[6912,256]{1,0:T(8,128)S(1)} fusion(f32[6912,32]{0,1:T(8,128)} %convolution_bitcast_fusion, f32[256,32]{1,0:T(8,128)S(1)} %copy-done.20), kind=kOutput, calls=%fused_computation.282 | convolution fusion | flops 679477248 | bytes 7995392 | tf_op jit(solution)/shard_map/rq,cq->rc/dot_general | solution.py:87
  462.9 5.9 %fusion.7 = bf16[1,6912,256]{2,1,0:T(8,128)(2,1)} fusion(f32[6912,256]{1,0:T(8,128)} %get-tuple-element.8, f32[6912,256]{1,0:T(8,128)S(1)} %fusion.168), kind=kLoop, calls=%fused_computation.22 | loop fusion | flops 5308416 | bytes 17694720 | tf_op jit(solution)/shard_map/stack | solution.py:91
  468.8 6.7 %maximum_bitcast_fusion = bf16[1,1,2,6912,256]{4,3,2,1,0:T(8,128)(2,1)} fusion(bf16[1,6912,256]{2,1,0:T(8,128)(2,1)} %fusion.7, bf16[1,6912,256]{2,1,0:T(8,128)(2,1)} %fusion.6), kind=kLoop, calls=%fused_computation.11 | loop fusion | flops 3538944 | bytes 14155776 | tf_op jit(solution)/shard_map/broadcast_in_dim | solution.py:91
  (150 shorter events, 35.7 us)
Async XLA Ops:
  7.2 245.7 %all-reduce.8.cloned.1.call-start = ((), (), s32[]{:S(2)}) async-start(), calls=%async_computation.1 | async-start | bytes 3538944 | tf_op jit(solution)/shard_map/psum | solution.py:50
  10.7 14.0 %collective-permute-start = (bf16[3,1,16,32,256]{4,3,2,1,0:T(8,128)(2,1)S(1)}, bf16[3,1,16,32,256]{4,3,2,1,0:T(8,128)(2,1)S(1)}, u32[]{:S(2)}, u32[]{:S(2)}) collective-permute-start(bf16[3,1,16,32,256]{4,3,2,1,0:T(8,128)(2,1)S(1)} %get-tuple-element.15), channel_id=1, source_target_pairs={{0,1},{1,2},{2,3},{3,4},{4,5},{5,6},{6,7},{7,8},{8,9},{9,10},{10,1... | collective-permute-start | bytes 2359304 | tf_op jit(solution)/shard_map/ppermute | solution.py:14
  15.6 13.3 %collective-permute-start.1 = (bf16[3,1,16,32,256]{4,3,2,1,0:T(8,128)(2,1)S(1)}, bf16[3,1,16,32,256]{4,3,2,1,0:T(8,128)(2,1)S(1)}, u32[]{:S(2)}, u32[]{:S(2)}) collective-permute-start(bf16[3,1,16,32,256]{4,3,2,1,0:T(8,128)(2,1)S(1)} %get-tuple-element.16), channel_id=1, source_target_pairs={{1,0},{2,1},{3,2},{4,3},{5,4},{6,5},{7,6},{8,7},{9,8},{10,9},{11,1... | collective-permute-start | bytes 2359304 | tf_op jit(solution)/shard_map/ppermute | solution.py:15
  38.1 2.7 copy-start.3
  48.2 1.7 copy-start.4
  58.4 4.7 copy-start.18
  58.4 4.7 copy-start.19
  58.8 4.7 copy-start.17
  58.8 5.0 %copy-start.16 = (bf16[2,16,32,256]{3,2,1,0:T(8,128)(2,1)S(1)}, bf16[2,16,32,256]{3,2,1,0:T(8,128)(2,1)}, u32[]{:S(2)}) copy-start(bf16[2,16,32,256]{3,2,1,0:T(8,128)(2,1)} %get-tuple-element.41) | copy-start | bytes 1572868
  58.8 5.4 %copy-start.15 = (bf16[2,16,32,256]{3,2,1,0:T(8,128)(2,1)S(1)}, bf16[2,16,32,256]{3,2,1,0:T(8,128)(2,1)}, u32[]{:S(2)}) copy-start(bf16[2,16,32,256]{3,2,1,0:T(8,128)(2,1)} %get-tuple-element.40) | copy-start | bytes 1572868
  59.3 5.2 %copy-start.14 = (bf16[2,16,32,256]{3,2,1,0:T(8,128)(2,1)S(1)}, bf16[2,16,32,256]{3,2,1,0:T(8,128)(2,1)}, u32[]{:S(2)}) copy-start(bf16[2,16,32,256]{3,2,1,0:T(8,128)(2,1)} %get-tuple-element.39) | copy-start | bytes 1572868
  59.4 5.6 %copy-start.13 = (bf16[2,16,32,256]{3,2,1,0:T(8,128)(2,1)S(1)}, bf16[2,16,32,256]{3,2,1,0:T(8,128)(2,1)}, u32[]{:S(2)}) copy-start(bf16[2,16,32,256]{3,2,1,0:T(8,128)(2,1)} %get-tuple-element.38) | copy-start | bytes 1572868
  59.4 5.9 %copy-start.12 = (bf16[2,16,32,256]{3,2,1,0:T(8,128)(2,1)S(1)}, bf16[2,16,32,256]{3,2,1,0:T(8,128)(2,1)}, u32[]{:S(2)}) copy-start(bf16[2,16,32,256]{3,2,1,0:T(8,128)(2,1)} %get-tuple-element.37) | copy-start | bytes 1572868
  59.7 5.9 %copy-start.11 = (bf16[2,16,32,256]{3,2,1,0:T(8,128)(2,1)S(1)}, bf16[2,16,32,256]{3,2,1,0:T(8,128)(2,1)}, u32[]{:S(2)}) copy-start(bf16[2,16,32,256]{3,2,1,0:T(8,128)(2,1)} %get-tuple-element.36) | copy-start | bytes 1572868
  59.7 6.3 %copy-start.10 = (bf16[2,16,32,256]{3,2,1,0:T(8,128)(2,1)S(1)}, bf16[2,16,32,256]{3,2,1,0:T(8,128)(2,1)}, u32[]{:S(2)}) copy-start(bf16[2,16,32,256]{3,2,1,0:T(8,128)(2,1)} %get-tuple-element.35) | copy-start | bytes 1572868
  60.1 3.0 copy-start.1
  60.1 6.2 %copy-start.9 = (bf16[2,16,32,256]{3,2,1,0:T(8,128)(2,1)S(1)}, bf16[2,16,32,256]{3,2,1,0:T(8,128)(2,1)}, u32[]{:S(2)}) copy-start(bf16[2,16,32,256]{3,2,1,0:T(8,128)(2,1)} %get-tuple-element.34) | copy-start | bytes 1572868
  60.1 6.6 %copy-start.8 = (bf16[2,16,32,256]{3,2,1,0:T(8,128)(2,1)S(1)}, bf16[2,16,32,256]{3,2,1,0:T(8,128)(2,1)}, u32[]{:S(2)}) copy-start(bf16[2,16,32,256]{3,2,1,0:T(8,128)(2,1)} %get-tuple-element.33) | copy-start | bytes 1572868
  63.4 3.7 copy-start.7
  63.8 3.7 copy-start.6
  64.2 3.6 copy-start.5
  72.8 2.8 copy-start
  75.6 6.1 %copy-start.21 = (f32[2,256,32]{1,2,0:T(8,128)S(1)}, f32[2,256,32]{1,2,0:T(8,128)}, u32[]{:S(2)}) copy-start(f32[2,256,32]{1,2,0:T(8,128)} %param.13) | copy-start | bytes 196612
  100.8 342.3 %all-reduce.6.cloned.1.call-start = ((), (), s32[]{:S(2)}) async-start(), calls=%async_computation | async-start | bytes 524288 | tf_op jit(solution)/shard_map/psum | solution.py:52
  255.1 35.7 %slice-start = ((s8[7077888]{0:T(1024)(128)(4,1)}), s8[2883584]{0:T(1024)(128)(4,1)S(1)}, s32[]{:S(2)}) async-start(s8[7077888]{0:T(1024)(128)(4,1)} %bitcast.643), calls=%async_computation.2 | async-start | bytes 5767168
  276.1 14.7 %copy-start.2 = (f32[6912,32]{0,1:T(8,128)}, f32[6912,32]{0,1:T(8,128)S(1)}, u32[]{:S(2)}) copy-start(f32[6912,32]{0,1:T(8,128)S(1)} %convolution_bitcast_fusion.1) | copy-start | bytes 2654212
  276.1 14.7 %slice-start.1 = ((s8[7077888]{0:T(1024)(128)(4,1)}), s8[4194304]{0:T(1024)(128)(4,1)S(1)}, s32[]{:S(2)}) async-start(s8[7077888]{0:T(1024)(128)(4,1)} %bitcast.643), calls=%async_computation.3 | async-start | bytes 8388608
  450.2 5.8 %copy-start.20 = (f32[256,32]{1,0:T(8,128)S(1)}, f32[256,32]{1,0:T(8,128)}, u32[]{:S(2)}) copy-start(f32[256,32]{1,0:T(8,128)} %get-tuple-element.5) | copy-start | bytes 98308
Sparse Core Ops, SparseCore 0:
  100.9 151.8 all-reduce.7
  302.8 140.2 all-reduce.5
where the time goes:
time: 489 us; the launch traced here: 483 us
  waiting for transfers between devices  283 us (58%)
  matrix products  93.2 us (19%)
  other arithmetic  66 us (13%)
  local copies, waits for them, and re-layouts  18.9 us (4%)
  between operations  15.3 us (3%)
  starting transfers between devices  6.94 us (1%)
    psum x1, waiting for transfers between devices, compress(): q_sum = lax.psum(right_terms(matrix, p_hat), ('dp', 'slab'))  140 us
    psum x1, waiting for transfers between devices, compress(): p_sum = lax.psum(left_terms(matrix, q_one), ('dp', 'slab'))  138 us
    dot_general x2, matrix products, right_terms(): jnp.einsum('rc,rq->cq', matrix, p_hat, precision=lax.Precision.HIGHEST)  26.4 us
    add x2, other arithmetic, per_device(): local_grads(act_pad, cot_rows, depth, height, width) + error_second  19.9 us
    dot_general x54, matrix products, local_grads(): jnp.einsum('nc,nd->cd', piece, out_rows, preferred_element_type=jnp.float32)  19 us
    dot_general x2, matrix products, left_terms(): jnp.einsum('rc,cq->rq', matrix, q_one, precision=lax.Precision.HIGHEST)  15.2 us
    another operation x2, other arithmetic, per_device(): new_error = jnp.stack([new_first, new_second])[None, None]  11.7 us
  transfers between devices with their start and end apart: 4, of which 3 were waited for; matrix products, arithmetic and copies ran while one was open for 4% of the time, Pallas kernels for 0%

commit v1 on v0

v1 whole, which is shorter than its diff:
```python
import functools

import jax
import jax.numpy as jnp
from jax import lax
from jax.experimental import pallas as pl
from jax.experimental.pallas import tpu as pltpu
from jax.sharding import PartitionSpec as P

BF, F32 = jnp.bfloat16, jnp.float32
MESH = pl.DeviceIdType.MESH
NT = (((1,), (1,)), ((), ()))
TN = (((0,), (0,)), ((), ()))
NN = (((1,), (0,)), ((), ()))
C, RANK, CELLS, WW, ROWS = 256, 32, 512, 32, 6912
PAD = CELLS + 2 * WW
HALF = ROWS // 2
QUART = 896


def mm(x, y, dims=NN):
    return lax.dot_general(x, y, dims, preferred_element_type=F32)


def split(x):
    hi = x.astype(BF)
    return hi, (x - hi.astype(F32)).astype(BF)


def precise(x, y, dims=NN):
    xh, xl = split(x)
    yh, yl = split(y)
    return mm(xh, yh, dims) + (mm(xh, yl, dims) + mm(xl, yh, dims))


def store_shifts(dst, plane, x):
    w = lax.broadcasted_iota(jnp.int32, (CELLS, C), 0) % WW
    wide = x.astype(F32)
    up = jnp.where(w == WW - 1, 0.0, pltpu.roll(wide, CELLS - 1, 0))
    down = jnp.where(w == 0, 0.0, pltpu.roll(wide, 1, 0))
    zero = jnp.zeros((WW, C), BF)
    for c, piece in enumerate((up.astype(BF), x, down.astype(BF))):
        dst[c, plane, 0:WW, :] = zero
        dst[c, plane, WW : WW + CELLS, :] = piece
        dst[c, plane, WW + CELLS : PAD, :] = zero


class Places:
    def __init__(self):
        self.y = lax.axis_index("dp")
        self.s = lax.axis_index("slab")
        self.x = self.s // 8
        self.z = (self.s // 2) % 4
        self.core = self.s % 2

    def at(self, dy, dx, dz, dcore=0):
        y = (self.y + dy) % 4
        x = (self.x + dx) % 4
        z = (self.z + dz) % 4
        core = (self.core + dcore) % 2
        return {"dp": y, "slab": x * 8 + z * 2 + core}

    def slab(self, step):
        return {"dp": self.y, "slab": (self.s + step + 32) % 32}


def main_kernel(
    pre_hbm, cot_hbm, vol_hbm, ker_hbm, err_hbm, qt_ref,
    mat_hbm, left_hbm, right_out,
    act, cot, vol, ker, err, cv, gv, bq, mat, send, r0, r1, a1, r2, r3, g2, fin, flat,
    srcv, sall, inv, local_sem, halo_send, halo_recv, ar_send, ar_recv, s_send, s_recv,
):
    me = Places()
    s, core = me.s, me.core

    loads = []
    for i, (src, dst) in enumerate(
        (
            (cot_hbm, cot.at[1:3]),
            (err_hbm.at[1], err.at[1]),
            (pre_hbm, act.at[1:3]),
            (err_hbm.at[0], err.at[0]),
            (ker_hbm, ker),
            (vol_hbm, vol.at[1:3]),
        )
    ):
        copy = pltpu.make_async_copy(src, dst, local_sem.at[i])
        copy.start()
        loads.append(copy)

    barrier = pltpu.get_barrier_semaphore()
    peers = [me.slab(-1), me.slab(1), me.at(0, 0, 0, 1)]
    for i in range(1, 4):
        peers += [me.at(i, 0, 0), me.at(0, i, 0), me.at(0, 0, i)]
    for peer in peers:
        pl.semaphore_signal(barrier, inc=1, device_id=peer, device_id_type=MESH)
    pl.semaphore_wait(barrier, len(peers))

    halos = []
    for i, (src, dst) in enumerate(((cot_hbm, cot), (pre_hbm, act), (vol_hbm, vol))):
        pair = []
        for j, (plane, slot, step) in enumerate(((1, 0, 1), (0, 3, -1))):
            copy = pltpu.make_async_remote_copy(
                src_ref=src.at[plane], dst_ref=dst.at[slot],
                send_sem=halo_send.at[i, j], recv_sem=halo_recv.at[i, j],
                device_id=me.slab(step), device_id_type=MESH,
            )
            copy.start()
            pair.append(copy)
        halos.append(pair)

    def wait_halo(i):
        for copy in halos[i]:
            copy.wait()

    def masked(ref, plane):
        if plane == 0:
            return jnp.where(s > 0, ref[0], jnp.zeros((CELLS, C), BF))
        if plane == 3:
            return jnp.where(s < 31, ref[3], jnp.zeros((CELLS, C), BF))
        return ref[plane]

    q2 = [jnp.concatenate(split(qt_ref[l]), 0) for l in range(2)]

    def lanes_of(k):
        if k < 13:
            return ((0, k * 256, 0, 256),)
        if k == 13:
            return ((0, k * 256, 0, 128), (1, 0, 128, 256))
        return ((1, k * 256 - HALF, 0, 256),)

    def put_left(l, k, value, add):
        for g in range(4):
            for lh, lane, lo, hi in lanes_of(k):
                where = (l, g // 2, g % 2 * 2 + lh, slice(None), slice(lane, lane + hi - lo))
                piece = value[8 * g : 8 * g + 8, lo:hi]
                send[where] = send[where] + piece if add else piece

    def error_left(l):
        for k in range(27):
            t = mm(q2[l], err[l, k * 256 : (k + 1) * 256, :], NT)
            put_left(l, k, t[:RANK] + t[RANK:], False)

    def right_factor(l, source, first):
        for d in range(2):
            parts = []
            for c in range(3):
                t = mm(source[c, first + d, WW : WW + CELLS, :], q2[l], NT)
                parts += list(split(t[:, :RANK] + t[:, RANK:]))
            bq[l, d, 0:WW, :] = jnp.zeros((WW, 6 * RANK), BF)
            bq[l, d, WW : WW + CELLS, :] = jnp.concatenate(parts, 1)
            bq[l, d, WW + CELLS : PAD, :] = jnp.zeros((WW, 6 * RANK), BF)

    def grad_left(l, planes):
        for a in range(3):
            for b in range(3):
                r = (2 - b) * WW
                x = bq[l, :, r : r + CELLS, :].reshape(2 * CELLS, 6 * RANK)
                t = mm(x, planes[a : a + 2].reshape(2 * CELLS, C), TN)
                for c in range(3):
                    piece = t[64 * c : 64 * c + 32] + t[64 * c + 32 : 64 * c + 64]
                    put_left(l, 9 * a + 3 * b + c, piece, True)

    one = 1 - core
    i1 = me.y * one + me.x * core
    i2 = me.x * one + me.z * core
    i3 = me.z * one + me.y * core

    def axis_peer(axis, i):
        if axis == 1:
            return me.at(i * one, i * core, 0)
        if axis == 2:
            return me.at(0, i * one, i * core)
        return me.at(i * core, 0, i * one)

    pending = []

    def push(src, dst, sems, l, n, peer):
        copy = pltpu.make_async_remote_copy(
            src_ref=src, dst_ref=dst, send_sem=sems[0].at[l, n], recv_sem=sems[1].at[l, n],
            device_id=peer, device_id_type=MESH,
        )
        copy.start()
        pending.append(copy)
        return copy

    ar_sems = (ar_send, ar_recv)

    def all_reduce(l):
        copy = push(send.at[l, one], r0.at[l], ar_sems, l, 0, me.at(0, 0, 0, 1))
        yield
        copy.wait_recv()
        for j in range(4):
            send[l, core, j] = send[l, core, j] + r0[l, j]
        copies = [
            push(send.at[l, core, (i1 + i) % 4], r1.at[l, i - 1], ar_sems, l, i, axis_peer(1, i))
            for i in range(1, 4)
        ]
        yield
        for copy in copies:
            copy.wait_recv()
        total = send[l, core, i1] + r1[l, 0] + r1[l, 1] + r1[l, 2]
        for j in range(3):
            a1[l, j] = total[:, QUART * j : QUART * (j + 1)]
        a1[l, 3] = jnp.concatenate([total[:, QUART * 3 :], jnp.zeros((8, 128), F32)], 1)
        copies = [
            push(a1.at[l, (i2 + i) % 4], r2.at[l, i - 1], ar_sems, l, 3 + i, axis_peer(2, i))
            for i in range(1, 4)
        ]
        yield
        for copy in copies:
            copy.wait_recv()
        r3[l, i3] = a1[l, i2] + r2[l, 0] + r2[l, 1] + r2[l, 2]
        copies = [
            push(r3.at[l, i3], r3.at[l, i3], ar_sems, l, 6 + i, axis_peer(3, i))
            for i in range(1, 4)
        ]
        yield
        for copy in copies:
            copy.wait_recv()
        g2[l, i2] = r3[l, 0] + r3[l, 1] + r3[l, 2] + r3[l, 3]
        copies = [
            push(g2.at[l, i2], g2.at[l, i2], ar_sems, l, 9 + i, axis_peer(2, i))
            for i in range(1, 4)
        ]
        yield
        for copy in copies:
            copy.wait_recv()
        for j in range(3):
            fin[l, core, i1, :, QUART * j : QUART * (j + 1)] = g2[l, j]
        fin[l, core, i1, :, QUART * 3 : HALF] = g2[l, 3, :, : HALF - 3 * QUART]
        copies = [
            push(
                fin.at[l, core, i1], fin.at[l, core, i1], ar_sems, l, 12 + i, axis_peer(1, i)
            )
            for i in range(1, 4)
        ]
        yield
        for copy in copies:
            copy.wait_recv()
        copy = push(fin.at[l, core], fin.at[l, core], ar_sems, l, 16, me.at(0, 0, 0, 1))
        yield
        copy.wait_recv()
        for h in range(2):
            for lh in range(2):
                hi, lo = split(jnp.concatenate([fin[l, h, lh], fin[l, h, 2 + lh]], 0))
                lanes = slice(HALF * lh, HALF * (lh + 1))
                flat[l, 16 * h : 16 * h + 16, lanes] = hi
                flat[l, RANK + 16 * h : RANK + 16 * h + 16, lanes] = lo
        yield

    def grad_step(l, planes, source, first, i):
        b, c = i // 3, i % 3
        r = (2 - b) * WW
        right = source[c, first : first + 2, r : r + CELLS, :].reshape(2 * CELLS, C)
        for a in range(3):
            rows = slice((9 * a + i) * 256, (9 * a + i + 1) * 256)
            g = mm(planes[a : a + 2].reshape(2 * CELLS, C), right, TN)
            mat[l, rows, :] = g + err[l, rows, :].astype(F32)

    loads[0].wait()
    for plane in (1, 2):
        store_shifts(cv, plane, cot[plane])
    loads[1].wait()
    error_left(1)
    right_factor(1, cv, 1)
    loads[3].wait()
    error_left(0)
    wait_halo(0)
    for plane in (0, 3):
        store_shifts(cv, plane, masked(cot, plane))
    loads[2].wait()
    wait_halo(1)
    for plane in range(4):
        act[plane] = jnp.maximum(masked(act, plane), jnp.zeros((CELLS, C), BF))
    grad_left(1, act)
    second = all_reduce(1)
    next(second)

    loads[4].wait()
    for d in range(2):
        total = None
        for a in range(3):
            x = jnp.concatenate(
                [
                    cv[c, d + 2 - a, (2 - b) * WW : (2 - b) * WW + CELLS, :]
                    for b in range(3)
                    for c in range(3)
                ],
                1,
            )
            w = jnp.concatenate([ker[9 * a + i] for i in range(9)], 1)
            t = mm(x, w, NT)
            total = t if total is None else total + t
        gate = jnp.where(act[1 + d] > 0, total, 0.0).astype(BF)
        store_shifts(gv, d, gate)
        next(second)
    right_factor(0, gv, 0)
    loads[5].wait()
    wait_halo(2)
    for plane in (0, 3):
        vol[plane] = masked(vol, plane)
    next(second)
    grad_left(0, vol)
    next(second)
    first = all_reduce(0)
    next(first)

    for i in range(9):
        grad_step(1, act, cv, 1, i)
        if i in (2, 5, 8):
            next(second)
            next(first)
    stores = [pltpu.make_async_copy(mat.at[1], mat_hbm.at[1], local_sem.at[6])]
    stores[0].start()
    for i in range(9):
        grad_step(0, vol, gv, 0, i)
        if i in (2, 5, 8):
            next(first)
    stores.append(pltpu.make_async_copy(mat.at[0], mat_hbm.at[0], local_sem.at[7]))
    stores[1].start()

    def right_terms(l):
        acc = jnp.zeros((RANK, C), F32)
        gram = jnp.zeros((2 * RANK, 2 * RANK), F32)
        for k in range(27):
            mh, ml = split(mat[l, k * 256 : (k + 1) * 256, :])
            both = flat[l, :, k * 256 : (k + 1) * 256]
            t = mm(both, mh)
            acc = acc + (t[:RANK] + (t[RANK:] + mm(both[:RANK], ml)))
            gram = gram + mm(both, both, NT)
        srcv[l] = acc
        return (gram[:RANK, :RANK] + gram[RANK:, RANK:]) + (
            gram[:RANK, RANK:] + gram[RANK:, :RANK]
        )

    gram_second = right_terms(1)
    next(first)
    gram_first = right_terms(0)
    left_copy = pltpu.make_async_copy(flat, left_hbm, local_sem.at[8])
    left_copy.start()

    s_sems = (s_send, s_recv)
    copy = push(srcv.at[one], sall.at[0, 0], s_sems, 0, 0, me.at(0, 0, 0, 1))
    eye = (
        lax.broadcasted_iota(jnp.int32, (RANK, RANK), 0)
        == lax.broadcasted_iota(jnp.int32, (RANK, RANK), 1)
    ).astype(F32)
    tables = [jnp.concatenate([g, eye], 1) for g in (gram_first, gram_second)]
    rows = lax.broadcasted_iota(jnp.int32, (RANK, 2 * RANK), 0)

    def eliminate(j0, j1):
        for j in range(j0, j1):
            for l in range(2):
                t = tables[l]
                row = t[j : j + 1, :] * (1.0 / t[j : j + 1, j : j + 1])
                tables[l] = jnp.where(rows == j, row, t - t[:, j : j + 1] * row)

    eliminate(0, 8)
    copy.wait_recv()
    mine = srcv[core] + sall[0, 0]
    for n, (index, step) in enumerate(((me.y, (1, 0, 0)), (me.x, (0, 1, 0)), (me.z, (0, 0, 1)))):
        sall[1 + n, index] = mine
        copies = [
            push(
                sall.at[1 + n, index], sall.at[1 + n, index], s_sems, 1 + n, i,
                me.at(*(i * v for v in step)),
            )
            for i in range(1, 4)
        ]
        eliminate(8 + 8 * n, 16 + 8 * n)
        for copy in copies:
            copy.wait_recv()
        mine = (sall[1 + n, 0] + sall[1 + n, 1]) + (sall[1 + n, 2] + sall[1 + n, 3])
    inv[core] = mine
    copy = push(inv.at[core], inv.at[core], s_sems, 4, 0, me.at(0, 0, 0, 1))
    copy.wait_recv()
    for l in range(2):
        right_out[l] = precise(tables[l][:, RANK:], inv[l])

    for copy in pending:
        copy.wait_send()
    for copy in stores:
        copy.wait()
    left_copy.wait()


def last_kernel(start_ref, mat_ref, left_ref, right_ref, err_out, sum_out, span):
    l, i = pl.program_id(0), pl.program_id(1)
    wh, wl = split(right_ref[l])
    right = jnp.concatenate([wl, wh, wh], 0)

    def product(lane, width):
        both = left_ref[l, :, pl.ds(lane, width)]
        return mm(jnp.concatenate([both[:RANK], both], 0), right, TN)

    width = mat_ref.shape[1]
    lane = pl.multiple_of(i * width, 256)
    err_out[0] = (mat_ref[0] - product(lane, width) * (1.0 / 128)).astype(BF)

    @pl.when(i == 0)
    def _():
        start = start_ref[0]
        base = jnp.minimum(start // 256, 25) * 256
        span[...] = product(pl.multiple_of(base, 256), 512)
        sum_out[l] = span[pl.ds(pl.multiple_of(start - base, 8), 216), :]


def per_device(volume, pre_act, cotangent, kernel_second, q_start, error):
    def rows(x):
        return x.reshape(2, CELLS, C)

    any_spec = pl.BlockSpec(memory_space=pl.ANY)
    vmem = pl.BlockSpec(memory_space=pltpu.VMEM)
    dma = pltpu.SemaphoreType.DMA
    V = pltpu.VMEM
    mat, left, right = pl.pallas_call(
        main_kernel,
        out_shape=(
            jax.ShapeDtypeStruct((2, ROWS, C), F32),
            jax.ShapeDtypeStruct((2, 2 * RANK, ROWS), BF),
            jax.ShapeDtypeStruct((2, RANK, C), F32),
        ),
        in_specs=[any_spec] * 5 + [vmem],
        out_specs=(any_spec, any_spec, vmem),
        scratch_shapes=[
            V((4, CELLS, C), BF), V((4, CELLS, C), BF), V((4, CELLS, C), BF),
            V((27, C, C), BF), V((2, ROWS, C), BF),
            V((3, 4, PAD, C), BF), V((3, 2, PAD, C), BF), V((2, 2, PAD, 6 * RANK), BF),
            V((2, ROWS, C), F32),
            V((2, 2, 4, 8, HALF), F32), V((2, 4, 8, HALF), F32), V((2, 3, 8, HALF), F32),
            V((2, 4, 8, QUART), F32), V((2, 3, 8, QUART), F32), V((2, 4, 8, QUART), F32),
            V((2, 4, 8, QUART), F32), V((2, 2, 4, 8, HALF), F32), V((2, 2 * RANK, ROWS), BF),
            V((2, RANK, C), F32), V((4, 4, RANK, C), F32), V((2, RANK, C), F32),
            dma((9,)), dma((3, 2)), dma((3, 2)), dma((2, 17)), dma((2, 17)),
            dma((5, 4)), dma((5, 4)),
        ],
        compiler_params=pltpu.CompilerParams(
            collective_id=0, has_side_effects=True, vmem_limit_bytes=60 << 20
        ),
        name="main_kernel",
    )(
        rows(pre_act), rows(cotangent), rows(volume), kernel_second,
        error.reshape(2, ROWS, C), jnp.swapaxes(q_start, 1, 2),
    )
    start = (lax.axis_index("slab") * (ROWS // 32)).astype(jnp.int32).reshape(1)
    width = 768
    new_error, summed = pl.pallas_call(
        last_kernel,
        grid=(2, ROWS // width),
        out_shape=(
            jax.ShapeDtypeStruct((2, ROWS, C), BF),
            jax.ShapeDtypeStruct((2, ROWS // 32, C), F32),
        ),
        in_specs=[
            pl.BlockSpec(memory_space=pltpu.SMEM),
            pl.BlockSpec((1, width, C), lambda l, i: (l, i, 0)),
            vmem,
            vmem,
        ],
        out_specs=(
            pl.BlockSpec((1, width, C), lambda l, i: (l, i, 0)),
            pl.BlockSpec((2, ROWS // 32, C), lambda l, i: (0, 0, 0)),
        ),
        scratch_shapes=[V((512, C), F32)],
        compiler_params=pltpu.CompilerParams(vmem_limit_bytes=32 << 20),
        name="last_kernel",
    )(start, mat, left, right)
    return (summed, new_error.reshape(1, 1, 2, ROWS, C))


def solution(mesh):
    in_specs = (
        P("dp", "slab", None, None, None),
        P("dp", "slab", None, None, None),
        P("dp", "slab", None, None, None),
        P(),
        P(),
        P("dp", "slab", None, None, None),
    )
    out_specs = (P(None, "slab", None), P("dp", "slab", None, None, None))
    return jax.shard_map(
        per_device, mesh=mesh, in_specs=in_specs, out_specs=out_specs, check_vma=False
    )
```

time: 489 us -> 108 us (0.22); the launches traced: 483 us -> 108 us
  waiting for transfers between devices: 283 us -> 0 us
  Pallas kernels: 0 us -> 99.7 us
  matrix products: 93.2 us -> 0 us
  other arithmetic: 66 us -> 0 us
  between operations: 15.3 us -> 0.65 us
  local copies, waits for them, and re-layouts: 18.9 us -> 7.33 us
  starting transfers between devices: 6.94 us -> 0 us
    psum x2 -> x0, waiting for transfers between devices: 279 us -> none  [the longest x1 140 us: compress(): q_sum = lax.psum(right_terms(matrix, p_hat), ('dp', 'slab'))]
    pallas_call x0 -> x2, Pallas kernels: none -> 99.7 us  [the longest x1 89.4 us: per_device(): pl.pallas_call(main_kernel, out_shape=(jax.ShapeDtypeStruct((2, ROWS, C),...]
    dot_general x89 -> x0, matrix products: 88.1 us -> none  [the longest x2 26.4 us: right_terms(): jnp.einsum('rc,rq->cq', matrix, p_hat, precision=lax.Precision.HIGHEST)]
    another operation x13 -> x0, other arithmetic: 25.9 us -> none  [the longest x2 11.7 us: per_device(): new_error = jnp.stack([new_first, new_second])[None, None]]
    add x3 -> x0, other arithmetic: 23.8 us -> none  [the longest x2 19.9 us: per_device(): local_grads(act_pad, cot_rows, depth, height, width) + error_second]
    slice x4 -> x0, local copies, waits for them, and re-layouts: 9.7 us -> none  [the longest x3 9.5 us: tap_rows(): padded[start_a:start_a + depth, start_b:start_b + height, start_c:start_c...]
    convert_element_type x2 -> x0, other arithmetic: 7.27 us -> none  [the longest x1 7.08 us: per_device(): error_second = error[0, 0, 1].astype(jnp.float32)]
    ppermute x2 -> x0, starting transfers between devices: 6.86 us -> none  [the longest x1 4.94 us: padded_2(): before = lax.ppermute(last, axis, up)]
  transfers between devices with their start and end apart: 4 -> 0, of which waited for: 3 -> 0; matrix products, arithmetic and copies ran while one was open for 4% -> 0% of each run, Pallas kernels for 0% -> 0%
where the time goes in v1:
time: 108 us
  Pallas kernels  99.7 us (92%)
  local copies, waits for them, and re-layouts  7.33 us (7%)
    pallas_call x1, Pallas kernels, per_device(): pl.pallas_call(main_kernel, out_shape=(jax.ShapeDtypeStruct((2, ROWS, C),...  89.4 us
    pallas_call x1, Pallas kernels, per_device(): pl.pallas_call(last_kernel, grid=(2, ROWS // width), out_shape=(jax.Shape...  10.3 us
    unnamed x6, local copies, waits for them, and re-layouts  7.33 us

profile of v1, /device:TPU:1, one launch (start us, length us, event | category | flops | bytes accessed | tf_op | source)
XLA Modules:
  0.0 107.7 jit_solution(11942836360749582658)
XLA Ops:
  0.6 89.4 %main_kernel.1 = (f32[2,6912,256]{2,1,0:T(8,128)}, bf16[2,64,6912]{2,1,0:T(8,128)(2,1)}, f32[2,32,256]{2,1,0:T(8,128)}) custom-call(bf16[2,512,256]{2,1,0:T(8,128)(2,1)} %bitcast.8, bf16[2,512,256]{2,1,0:T(8,128)(2,1)} %bitcast.9, bf16[2,512,256]{2,1,0:T(8,128)(2,1)} %bitcast.10, bf16[27,256,256]{2,1,0:T(8,128)(2,1)} %ker_hbm.1, ...), custom_call_target="tpu_custom_call" | custom-call | tf_op jit(solution)/shard_map/main_kernel/pallas_call | solution.py:417
  90.0 0.0 copy-start
  90.0 5.0 %copy-done = f32[2,6912,256]{2,1,0:T(8,128)S(1)} copy-done((f32[2,6912,256]{2,1,0:T(8,128)S(1)}, f32[2,6912,256]{2,1,0:T(8,128)}, u32[]{:S(2)}) %copy-start) | copy-done | bytes 14155800
  95.0 0.0 copy-start.1
  95.0 1.5 %copy-done.1 = bf16[2,64,6912]{2,1,0:T(8,128)(2,1)S(1)} copy-done((bf16[2,64,6912]{2,1,0:T(8,128)(2,1)S(1)}, bf16[2,64,6912]{2,1,0:T(8,128)(2,1)}, u32[]{:S(2)}) %copy-start.1) | copy-done | bytes 1769496
  96.5 0.0 copy-start.2
  96.5 0.8 copy-done.2
  97.3 10.3 %last_kernel.1 = (bf16[2,6912,256]{2,1,0:T(8,128)(2,1)}, f32[2,216,256]{2,1,0:T(8,128)}) custom-call(s32[1]{0:T(128)} %bitcast.start_ref, f32[2,6912,256]{2,1,0:T(8,128)S(1)} %copy-done, bf16[2,64,6912]{2,1,0:T(8,128)(2,1)S(1)} %copy-done.1, f32[2,32,256]{2,1,0:T(8,128)S(1)} %copy-done.2), custom_call_target="tpu_custom_call" | custom-call | tf_op jit(solution)/shard_map/last_kernel/pallas_call | solution.py:448
Async XLA Ops:
  90.0 5.0 %copy-start = (f32[2,6912,256]{2,1,0:T(8,128)S(1)}, f32[2,6912,256]{2,1,0:T(8,128)}, u32[]{:S(2)}) copy-start(f32[2,6912,256]{2,1,0:T(8,128)} %get-tuple-element.7.mat_ref) | copy-start | bytes 42467332
  95.0 1.5 %copy-start.1 = (bf16[2,64,6912]{2,1,0:T(8,128)(2,1)S(1)}, bf16[2,64,6912]{2,1,0:T(8,128)(2,1)}, u32[]{:S(2)}) copy-start(bf16[2,64,6912]{2,1,0:T(8,128)(2,1)} %get-tuple-element.8.left_ref) | copy-start | bytes 5308420
  96.5 0.8 copy-start.2

commit v2 on v1

v2 whole, which is shorter than its diff:
```python
import functools

import jax
import jax.numpy as jnp
from jax import lax
from jax.experimental import pallas as pl
from jax.experimental.pallas import tpu as pltpu
from jax.sharding import PartitionSpec as P

BF, F32 = jnp.bfloat16, jnp.float32
MESH = pl.DeviceIdType.MESH
NT = (((1,), (1,)), ((), ()))
TN = (((0,), (0,)), ((), ()))
NN = (((1,), (0,)), ((), ()))
C, RANK, CELLS, WW, ROWS = 256, 32, 512, 32, 6912
PAD = CELLS + 2 * WW
STEP = 9
MAIN_VMEM, LAST_VMEM = 42, 24


def mm(x, y, dims=NN):
    return lax.dot_general(x, y, dims, preferred_element_type=F32)


def split(x):
    hi = x.astype(BF)
    return hi, (x - hi.astype(F32)).astype(BF)


def precise(x, y, dims=NN):
    xh, xl = split(x)
    yh, yl = split(y)
    return mm(xh, yh, dims) + (mm(xh, yl, dims) + mm(xl, yh, dims))


def store_shifts(dst, plane, x):
    w = lax.broadcasted_iota(jnp.int32, (CELLS, C), 0) % WW
    wide = x.astype(F32)
    up = jnp.where(w == WW - 1, 0.0, pltpu.roll(wide, CELLS - 1, 0))
    down = jnp.where(w == 0, 0.0, pltpu.roll(wide, 1, 0))
    zero = jnp.zeros((WW, C), BF)
    for c, piece in enumerate((up.astype(BF), x, down.astype(BF))):
        dst[c, plane, 0:WW, :] = zero
        dst[c, plane, WW : WW + CELLS, :] = piece
        dst[c, plane, WW + CELLS : PAD, :] = zero


class Places:
    def __init__(self):
        self.y = lax.axis_index("dp")
        self.s = lax.axis_index("slab")
        self.x = self.s // 8
        self.z = (self.s // 2) % 4
        self.core = self.s % 2

    def at(self, dy, dx, dz, dcore=0):
        y = (self.y + dy) % 4
        x = (self.x + dx) % 4
        z = (self.z + dz) % 4
        core = (self.core + dcore) % 2
        return {"dp": y, "slab": x * 8 + z * 2 + core}

    def slab(self, step):
        return {"dp": self.y, "slab": (self.s + step + 32) % 32}


def main_kernel(
    pre_hbm, cot_hbm, vol_hbm, ker_hbm, err_hbm, qt_ref,
    mat, flat, right_out,
    act, cot, vol, ker, err, cv, gv, bq, acc, send, r0, r1, r2, fin,
    srcv, sall, inv, local_sem, halo_send, halo_recv, pair_send, pair_recv, ar_send, ar_recv,
    s_send, s_recv,
):
    me = Places()
    s, core = me.s, me.core
    one = 1 - core

    loads = []
    for i, (src, dst) in enumerate(
        (
            (cot_hbm, cot.at[1:3]),
            (ker_hbm, ker),
            (err_hbm.at[0], err.at[0]),
            (vol_hbm, vol.at[1:3]),
            (pre_hbm, act.at[1:3]),
            (err_hbm.at[1], err.at[1]),
        )
    ):
        copy = pltpu.make_async_copy(src, dst, local_sem.at[i])
        copy.start()
        loads.append(copy)

    barrier = pltpu.get_barrier_semaphore()
    peers = [me.slab(-1), me.slab(1), me.at(0, 0, 0, 1)]
    for i in range(1, 4):
        peers += [me.at(i, 0, 0), me.at(0, i, 0), me.at(0, 0, i)]
        peers += [me.at(i * one, j, i * core) for j in range(1, 4)]
    for peer in peers:
        pl.semaphore_signal(barrier, inc=1, device_id=peer, device_id_type=MESH)
    pl.semaphore_wait(barrier, len(peers))

    halos = []
    for i, (src, dst) in enumerate(((cot_hbm, cot), (vol_hbm, vol), (pre_hbm, act))):
        pair = []
        for j, (plane, slot, step) in enumerate(((1, 0, 1), (0, 3, -1))):
            copy = pltpu.make_async_remote_copy(
                src_ref=src.at[plane], dst_ref=dst.at[slot],
                send_sem=halo_send.at[i, j], recv_sem=halo_recv.at[i, j],
                device_id=me.slab(step), device_id_type=MESH,
            )
            copy.start()
            pair.append(copy)
        halos.append(pair)

    def wait_halo(i):
        for copy in halos[i]:
            copy.wait()

    def masked(ref, plane):
        if plane == 0:
            return jnp.where(s > 0, ref[0], jnp.zeros((CELLS, C), BF))
        if plane == 3:
            return jnp.where(s < 31, ref[3], jnp.zeros((CELLS, C), BF))
        return ref[plane]

    q2 = [jnp.concatenate(split(qt_ref[l]), 0) for l in range(2)]

    def error_left(l):
        for k in range(27):
            t = mm(q2[l], err[l, k * 256 : (k + 1) * 256, :], NT)
            send[l, k % 2, k // 2] = t[:RANK] + t[RANK:]
        for k in range(27, 32):
            send[l, k % 2, k // 2] = jnp.zeros((RANK, C), F32)

    def right_factor(l, source, first):
        for d in range(2):
            parts = []
            for c in range(3):
                t = mm(source[c, first + d, WW : WW + CELLS, :], q2[l], NT)
                parts += list(split(t[:, :RANK] + t[:, RANK:]))
            bq[l, d, 0:WW, :] = jnp.zeros((WW, 6 * RANK), BF)
            bq[l, d, WW : WW + CELLS, :] = jnp.concatenate(parts, 1)
            bq[l, d, WW + CELLS : PAD, :] = jnp.zeros((WW, 6 * RANK), BF)

    def grad_left(l, planes, a):
        for b in range(3):
            r = (2 - b) * WW
            x = bq[l, :, r : r + CELLS, :].reshape(2 * CELLS, 6 * RANK)
            t = mm(x, planes[a : a + 2].reshape(2 * CELLS, C), TN)
            for c in range(3):
                k = 9 * a + 3 * b + c
                piece = t[64 * c : 64 * c + 32] + t[64 * c + 32 : 64 * c + 64]
                send[l, k % 2, k // 2] = send[l, k % 2, k // 2] + piece

    i1 = me.y * one + me.x * core
    i2 = me.x * one + me.z * core
    i3 = me.z * one + me.y * core
    here = i1 * 4 + i2
    others = [(i, j) for i in range(4) for j in range(4) if i + j > 0]

    def plane_peer(i, j):
        return me.at(i * one, i * core + j * one, j * core)

    pending = []

    def push(src, dst, sems, l, n, peer):
        copy = pltpu.make_async_remote_copy(
            src_ref=src, dst_ref=dst, send_sem=sems[0].at[l, n], recv_sem=sems[1].at[l, n],
            device_id=peer, device_id_type=MESH,
        )
        copy.start()
        pending.append(copy)
        return copy

    ar_sems = (ar_send, ar_recv)
    pair_sems = (pair_send, pair_recv)
    bounds = (0, 4, 9, 14)

    def pair_step(l, n):
        part = pl.ds(bounds[n], bounds[n + 1] - bounds[n])
        return push(
            send.at[l, one, part], r0.at[l, part], pair_sems, l, n, me.at(0, 0, 0, 1)
        )

    def pair_add(l, n, copy):
        copy.wait_recv()
        for t in range(bounds[n], bounds[n + 1]):
            send[l, core, t] = send[l, core, t] + r0[l, t]

    def all_reduce(l):
        copies = [
            push(
                send.at[l, core, (i1 + i) % 4 * 4 + (i2 + j) % 4], r1.at[l, n],
                ar_sems, l, n, plane_peer(i, j),
            )
            for n, (i, j) in enumerate(others)
        ]
        yield
        total = send[l, core, here]
        for n, copy in enumerate(copies):
            copy.wait_recv()
            total = total + r1[l, n]
        r2[l, i3] = total
        copies = [
            push(
                r2.at[l, i3], r2.at[l, i3], ar_sems, l, 14 + i,
                me.at(i * core, 0, i * one),
            )
            for i in range(1, 4)
        ]
        yield
        for copy in copies:
            copy.wait_recv()
        fin[l, core, here] = (r2[l, 0] + r2[l, 1]) + (r2[l, 2] + r2[l, 3])
        copies = [
            push(
                fin.at[l, core, here], fin.at[l, core, here], ar_sems, l, 18 + n,
                plane_peer(i, j),
            )
            for n, (i, j) in enumerate(others)
        ]
        yield
        for copy in copies:
            copy.wait_recv()
        copy = push(
            fin.at[l, core, 0:14], fin.at[l, core, 0:14], pair_sems, l, 3, me.at(0, 0, 0, 1)
        )
        yield
        copy.wait_recv()
        yield

    def grad_step(l, planes, source, first, i):
        b, c = i // 3, i % 3
        r = (2 - b) * WW
        right = source[c, first : first + 2, r : r + CELLS, :].reshape(2 * CELLS, C)
        for a in range(3):
            rows = slice((9 * a + i) * 256, (9 * a + i + 1) * 256)
            g = mm(planes[a : a + 2].reshape(2 * CELLS, C), right, TN)
            mat[l, rows, :] = g + err[l, rows, :].astype(F32)

    def back_part(d, a):
        x = jnp.concatenate(
            [
                cv[c, d + 2 - a, (2 - b) * WW : (2 - b) * WW + CELLS, :]
                for b in range(3)
                for c in range(3)
            ],
            1,
        )
        w = jnp.concatenate([ker[9 * a + i] for i in range(9)], 1)
        return mm(x, w, NT)

    loads[0].wait()
    for plane in (1, 2):
        store_shifts(cv, plane, cot[plane])
    loads[1].wait()
    acc[0] = back_part(0, 0) + back_part(0, 1)
    acc[1] = back_part(1, 1) + back_part(1, 2)
    loads[2].wait()
    error_left(0)
    wait_halo(0)
    for plane in (0, 3):
        store_shifts(cv, plane, masked(cot, plane))
    loads[4].wait()
    for d in range(2):
        total = acc[d] + back_part(d, 2 - 2 * d)
        store_shifts(gv, d, jnp.where(act[1 + d] > 0, total, 0.0).astype(BF))
    right_factor(0, gv, 0)
    loads[3].wait()
    wait_halo(1)
    for plane in (0, 3):
        vol[plane] = masked(vol, plane)
    pairs = []
    for a in range(3):
        grad_left(0, vol, a)
        pairs.append(pair_step(0, a))
        if a > 0:
            pair_add(0, a - 1, pairs[a - 1])
    loads[5].wait()
    error_left(1)
    right_factor(1, cv, 1)
    pair_add(0, 2, pairs[2])
    first = all_reduce(0)
    next(first)
    wait_halo(2)
    for plane in range(4):
        act[plane] = jnp.maximum(masked(act, plane), jnp.zeros((CELLS, C), BF))
    pairs = []
    for a in range(3):
        grad_left(1, act, a)
        pairs.append(pair_step(1, a))
        if a > 0:
            pair_add(1, a - 1, pairs[a - 1])
    grad_step(0, vol, gv, 0, 0)
    grad_step(0, vol, gv, 0, 1)
    pair_add(1, 2, pairs[2])
    second = all_reduce(1)
    next(second)
    for i in range(2, 7):
        grad_step(0, vol, gv, 0, i)
    next(first)
    for i in range(7, 9):
        grad_step(0, vol, gv, 0, i)
    for i in range(0, 2):
        grad_step(1, act, cv, 1, i)
    next(second)
    for i in range(2, 5):
        grad_step(1, act, cv, 1, i)
    next(first)
    for i in range(5, 9):
        grad_step(1, act, cv, 1, i)
    next(second)
    next(first)

    def right_tap(l, k, hand, tap, sums):
        mh, ml = split(mat[l, pl.ds(pl.multiple_of(k * 256, 256), 256), :])
        both = jnp.concatenate(split(fin[l, hand, tap]), 0)
        flat[l, k] = both
        t = mm(both, mh)
        return (
            sums[0] + (t[:RANK] + (t[RANK:] + mm(both[:RANK], ml))),
            sums[1] + mm(both, both, NT),
        )

    def right_half(l, hand, sums):
        for t in range(13):
            sums = right_tap(l, 2 * t + hand, hand, t, sums)
        return sums

    def right_done(l, sums):
        srcv[l], gram = right_tap(l, 26, 0, 13, sums)
        return (gram[:RANK, :RANK] + gram[RANK:, RANK:]) + (
            gram[:RANK, RANK:] + gram[RANK:, :RANK]
        )

    zero = (jnp.zeros((RANK, C), F32), jnp.zeros((2 * RANK, 2 * RANK), F32))
    sums_first = right_half(0, core, zero)
    next(first)
    next(second)
    sums_first = right_half(0, one, sums_first)
    gram_first = right_done(0, sums_first)
    sums_second = right_half(1, core, zero)
    next(second)
    gram_second = right_done(1, right_half(1, one, sums_second))

    s_sems = (s_send, s_recv)
    copy = push(srcv.at[one], sall.at[0, 0], s_sems, 0, 0, me.at(0, 0, 0, 1))
    eye = (
        lax.broadcasted_iota(jnp.int32, (RANK, RANK), 0)
        == lax.broadcasted_iota(jnp.int32, (RANK, RANK), 1)
    ).astype(F32)
    tables = [jnp.concatenate([g, eye], 1) for g in (gram_first, gram_second)]
    rows = lax.broadcasted_iota(jnp.int32, (RANK, 2 * RANK), 0)

    def eliminate(j0, j1):
        for j in range(j0, j1):
            for l in range(2):
                t = tables[l]
                row = t[j : j + 1, :] * (1.0 / t[j : j + 1, j : j + 1])
                tables[l] = jnp.where(rows == j, row, t - t[:, j : j + 1] * row)

    eliminate(0, 8)
    copy.wait_recv()
    mine = srcv[core] + sall[0, 0]
    for n, (index, step) in enumerate(((me.y, (1, 0, 0)), (me.x, (0, 1, 0)), (me.z, (0, 0, 1)))):
        sall[1 + n, index] = mine
        copies = [
            push(
                sall.at[1 + n, index], sall.at[1 + n, index], s_sems, 1 + n, i,
                me.at(*(i * v for v in step)),
            )
            for i in range(1, 4)
        ]
        eliminate(8 + 8 * n, 16 + 8 * n)
        for copy in copies:
            copy.wait_recv()
        mine = (sall[1 + n, 0] + sall[1 + n, 1]) + (sall[1 + n, 2] + sall[1 + n, 3])
    inv[core] = mine
    copy = push(inv.at[core], inv.at[core], s_sems, 4, 0, me.at(0, 0, 0, 1))
    copy.wait_recv()
    for l in range(2):
        right_out[l] = precise(tables[l][:, RANK:], inv[l])

    for copy in pending:
        copy.wait_send()


def last_kernel(start_ref, mat_ref, left_ref, right_ref, err_out, sum_out, span):
    l, i = pl.program_id(0), pl.program_id(1)
    wh, wl = split(right_ref[l])
    right = jnp.concatenate([wl, wh, wh], 0)

    def product(k):
        both = left_ref[l, k]
        return mm(jnp.concatenate([both[:RANK], both], 0), right, TN)

    for j in range(STEP):
        k = i * STEP + j
        rows = pl.ds(pl.multiple_of(k * 256, 256), 256)
        value = mat_ref[l, rows, :] - product(k) * (1.0 / 128)
        err_out[0, j * 256 : (j + 1) * 256, :] = value.astype(BF)

    @pl.when(i == 0)
    def _():
        start = start_ref[0]
        k = jnp.minimum(start // 256, 25)
        span[0:256, :] = product(k)
        span[256:512, :] = product(k + 1)
        sum_out[l] = span[pl.ds(pl.multiple_of(start - k * 256, 8), 216), :]


def per_device(volume, pre_act, cotangent, kernel_second, q_start, error):
    def rows(x):
        return x.reshape(2, CELLS, C)

    hbm = pl.BlockSpec(memory_space=pltpu.HBM)
    vmem = pl.BlockSpec(memory_space=pltpu.VMEM)
    dma = pltpu.SemaphoreType.DMA
    V = pltpu.VMEM
    mat, left, right = pl.pallas_call(
        main_kernel,
        out_shape=(
            V((2, ROWS, C), F32),
            V((2, 27, 2 * RANK, C), BF),
            V((2, RANK, C), F32),
        ),
        in_specs=[hbm] * 5 + [vmem],
        out_specs=(vmem, vmem, vmem),
        scratch_shapes=[
            V((4, CELLS, C), BF), V((4, CELLS, C), BF), V((4, CELLS, C), BF),
            V((27, C, C), BF), V((2, ROWS, C), BF),
            V((3, 4, PAD, C), BF), V((3, 2, PAD, C), BF), V((2, 2, PAD, 6 * RANK), BF),
            V((2, CELLS, C), F32),
            V((2, 2, 16, RANK, C), F32), V((2, 14, RANK, C), F32), V((2, 15, RANK, C), F32),
            V((2, 4, RANK, C), F32), V((2, 2, 16, RANK, C), F32),
            V((2, RANK, C), F32), V((4, 4, RANK, C), F32), V((2, RANK, C), F32),
            dma((6,)), dma((3, 2)), dma((3, 2)), dma((2, 4)), dma((2, 4)), dma((2, 33)),
            dma((2, 33)), dma((5, 4)), dma((5, 4)),
        ],
        compiler_params=pltpu.CompilerParams(
            collective_id=0, has_side_effects=True, vmem_limit_bytes=MAIN_VMEM << 20
        ),
        name="main_kernel",
    )(
        rows(pre_act), rows(cotangent), rows(volume), kernel_second,
        error.reshape(2, ROWS, C), jnp.swapaxes(q_start, 1, 2),
    )
    start = (lax.axis_index("slab") * (ROWS // 32)).astype(jnp.int32).reshape(1)
    width = 256 * STEP
    new_error, summed = pl.pallas_call(
        last_kernel,
        grid=(2, 27 // STEP),
        out_shape=(
            jax.ShapeDtypeStruct((2, ROWS, C), BF),
            jax.ShapeDtypeStruct((2, ROWS // 32, C), F32),
        ),
        in_specs=[pl.BlockSpec(memory_space=pltpu.SMEM), vmem, vmem, vmem],
        out_specs=(
            pl.BlockSpec((1, width, C), lambda l, i: (l, i, 0)),
            pl.BlockSpec((2, ROWS // 32, C), lambda l, i: (0, 0, 0)),
        ),
        scratch_shapes=[V((512, C), F32)],
        compiler_params=pltpu.CompilerParams(vmem_limit_bytes=LAST_VMEM << 20),
        name="last_kernel",
    )(start, mat, left, right)
    return (summed, new_error.reshape(1, 1, 2, ROWS, C))


def solution(mesh):
    in_specs = (
        P("dp", "slab", None, None, None),
        P("dp", "slab", None, None, None),
        P("dp", "slab", None, None, None),
        P(),
        P(),
        P("dp", "slab", None, None, None),
    )
    out_specs = (P(None, "slab", None), P("dp", "slab", None, None, None))
    return jax.shard_map(
        per_device, mesh=mesh, in_specs=in_specs, out_specs=out_specs, check_vma=False
    )
```

time: 108 us -> 80.5 us (0.75)
  Pallas kernels: 99.7 us -> 79.7 us
  local copies, waits for them, and re-layouts: 7.33 us -> 0 us
    pallas_call x2, Pallas kernels: 99.7 us -> 79.7 us  [the longest x1 73.9 us: per_device(): pl.pallas_call(main_kernel, out_shape=(V((2, ROWS, C), F32), V((2, 27, 2...]
    unnamed x6 -> x0, local copies, waits for them, and re-layouts: 7.33 us -> none
where the time goes in v2:
time: 80.5 us; the launch traced here: 80.4 us
  Pallas kernels  79.7 us (99%)
    pallas_call x1, Pallas kernels, per_device(): pl.pallas_call(main_kernel, out_shape=(V((2, ROWS, C), F32), V((2, 27, 2...  73.9 us
    pallas_call x1, Pallas kernels, per_device(): pl.pallas_call(last_kernel, grid=(2, 27 // STEP), out_shape=(jax.ShapeDty...  5.79 us

profile of v2, /device:TPU:1, one launch (start us, length us, event | category | flops | bytes accessed | tf_op | source)
XLA Modules:
  0.0 80.4 jit_solution(5853336227508249339)
XLA Ops:
  0.6 73.9 %main_kernel.1 = (f32[2,6912,256]{2,1,0:T(8,128)S(1)}, bf16[2,27,64,256]{3,2,1,0:T(8,128)(2,1)S(1)}, f32[2,32,256]{2,1,0:T(8,128)S(1)}) custom-call(bf16[2,512,256]{2,1,0:T(8,128)(2,1)} %bitcast.8, bf16[2,512,256]{2,1,0:T(8,128)(2,1)} %bitcast.9, bf16[2,512,256]{2,1,0:T(8,128)(2,1)} %bitcast.10, bf16[27,256,256]{2,1,0:T(8,128)(2,1)} %ker_hbm.1, ...), custom_call_target="tpu_custom_call" | custom-call | tf_op jit(solution)/shard_map/main_kernel/pallas_call | solution.py:420
  74.6 5.8 %last_kernel.1 = (bf16[2,6912,256]{2,1,0:T(8,128)(2,1)}, f32[2,216,256]{2,1,0:T(8,128)}) custom-call(s32[1]{0:T(128)} %bitcast.start_ref, f32[2,6912,256]{2,1,0:T(8,128)S(1)} %get-tuple-element.7.mat_ref, bf16[2,27,64,256]{3,2,1,0:T(8,128)(2,1)S(1)} %get-tuple-element.8.left_ref, f32[2,32,256]{2,1,0:T(8,128)S(1)} %get-tuple-element.9.right_ref), custom_call_target="tpu_custom_call" | custom-call | tf_op jit(solution)/shard_map/last_kernel/pallas_call | solution.py:450

commit v3 on v2

v3 whole, which is shorter than its diff:
```python
import functools

import jax
import jax.numpy as jnp
from jax import lax
from jax.experimental import pallas as pl
from jax.experimental.pallas import tpu as pltpu
from jax.sharding import PartitionSpec as P

BF, F32 = jnp.bfloat16, jnp.float32
MESH = pl.DeviceIdType.MESH
NT = (((1,), (1,)), ((), ()))
TN = (((0,), (0,)), ((), ()))
NN = (((1,), (0,)), ((), ()))
C, RANK, CELLS, WW, ROWS = 256, 32, 512, 32, 6912
PAD = CELLS + 2 * WW
MAIN_VMEM, LAST_VMEM = 46, 16


def mm(x, y, dims=NN):
    return lax.dot_general(x, y, dims, preferred_element_type=F32)


def split(x):
    hi = x.astype(BF)
    return hi, (x - hi.astype(F32)).astype(BF)


def precise(x, y, dims=NN):
    xh, xl = split(x)
    yh, yl = split(y)
    return mm(xh, yh, dims) + (mm(xh, yl, dims) + mm(xl, yh, dims))


def store_shifts(dst, plane, x):
    w = lax.broadcasted_iota(jnp.int32, (CELLS, C), 0) % WW
    wide = x.astype(F32)
    up = jnp.where(w == WW - 1, 0.0, pltpu.roll(wide, CELLS - 1, 0))
    down = jnp.where(w == 0, 0.0, pltpu.roll(wide, 1, 0))
    zero = jnp.zeros((WW, C), BF)
    for c, piece in enumerate((up.astype(BF), x, down.astype(BF))):
        dst[c, plane, 0:WW, :] = zero
        dst[c, plane, WW : WW + CELLS, :] = piece
        dst[c, plane, WW + CELLS : PAD, :] = zero


class Places:
    def __init__(self):
        self.y = lax.axis_index("dp")
        self.s = lax.axis_index("slab")
        self.x = self.s // 8
        self.z = (self.s // 2) % 4
        self.core = self.s % 2

    def at(self, dy, dx, dz, dcore=0):
        y = (self.y + dy) % 4
        x = (self.x + dx) % 4
        z = (self.z + dz) % 4
        core = (self.core + dcore) % 2
        return {"dp": y, "slab": x * 8 + z * 2 + core}

    def slab(self, step):
        return {"dp": self.y, "slab": (self.s + step + 32) % 32}


def left_product(both, right):
    return mm(jnp.concatenate([both[:RANK], both], 0), right, TN) * (1.0 / 128)


def stacked_right(right):
    hi, lo = split(right)
    return jnp.concatenate([lo, hi, hi], 0)


def main_kernel(
    pre_hbm, cot_hbm, vol_hbm, ker_hbm, err_hbm, qt_ref,
    mat_first, flat, right_out, tail,
    act, cot, vol, ker, err, cv, gv, bq_first, bq_second, acc, gate, mat_second, send, r0, r1, r2, fin,
    srcv, sall, local_sem, halo_send, halo_recv, pair_send, pair_recv, ar_send, ar_recv,
    s_send, s_recv,
):
    me = Places()
    s, core = me.s, me.core
    one = 1 - core

    loads = []
    for i, (src, dst) in enumerate(
        (
            (cot_hbm, cot.at[1:3]),
            (pre_hbm, act.at[1:3]),
            (err_hbm.at[1], err.at[1]),
            (ker_hbm, ker),
            (err_hbm.at[0], err.at[0]),
            (vol_hbm, vol.at[1:3]),
        )
    ):
        copy = pltpu.make_async_copy(src, dst, local_sem.at[i])
        copy.start()
        loads.append(copy)

    barrier = pltpu.get_barrier_semaphore()
    peers = [me.slab(-1), me.slab(1)]
    for i in range(1, 4):
        peers += [me.at(i, 0, 0), me.at(0, i, 0)]
        for j in range(1, 4):
            peers += [me.at(i, j, 0), me.at(i * one, i * core, j)]
    peers += [me.at(0, 0, i // 2, i % 2) for i in range(1, 8)]
    for peer in peers:
        pl.semaphore_signal(barrier, inc=1, device_id=peer, device_id_type=MESH)
    halos = []

    def send_halos():
        for i, (src, dst) in enumerate(((cot_hbm, cot), (vol_hbm, vol), (pre_hbm, act))):
            pair = []
            for j, (plane, slot, step) in enumerate(((1, 0, 1), (0, 3, -1))):
                copy = pltpu.make_async_remote_copy(
                    src_ref=src.at[plane], dst_ref=dst.at[slot],
                    send_sem=halo_send.at[i, j], recv_sem=halo_recv.at[i, j],
                    device_id=me.slab(step), device_id_type=MESH,
                )
                copy.start()
                pair.append(copy)
            halos.append(pair)

    def wait_halo(i):
        for copy in halos[i]:
            copy.wait()

    def masked(ref, plane):
        if plane == 0:
            return jnp.where(s > 0, ref[0], jnp.zeros((CELLS, C), BF))
        if plane == 3:
            return jnp.where(s < 31, ref[3], jnp.zeros((CELLS, C), BF))
        return ref[plane]

    q2 = [jnp.concatenate(split(qt_ref[l]), 0) for l in range(2)]

    def error_left(l):
        for k in range(27):
            t = mm(q2[l], err[l, k * 256 : (k + 1) * 256, :], NT)
            send[l, k % 2, k // 2] = t[:RANK] + t[RANK:]
        for k in range(27, 32):
            send[l, k % 2, k // 2] = jnp.zeros((RANK, C), F32)

    def right_factor(l, dst, d, x):
        t = mm(x, q2[l], NT)
        t = t[:, :RANK] + t[:, RANK:]
        w = lax.broadcasted_iota(jnp.int32, (CELLS, RANK), 0) % WW
        up = jnp.where(w == WW - 1, 0.0, pltpu.roll(t, CELLS - 1, 0))
        down = jnp.where(w == 0, 0.0, pltpu.roll(t, 1, 0))
        zero = jnp.zeros((WW, 6 * RANK), BF)
        dst[d, 0:WW, :] = zero
        dst[d, WW : WW + CELLS, :] = jnp.concatenate([*split(up), *split(t), *split(down)], 1)
        dst[d, WW + CELLS : PAD, :] = zero

    def grad_left(l, a, factor, planes):
        size = planes.shape[0] * CELLS
        for b in range(3):
            r = (2 - b) * WW
            x = factor[:, r : r + CELLS, :].reshape(size, 6 * RANK)
            t = mm(x, planes[...].reshape(size, C), TN)
            for c in range(3):
                k = 9 * a + 3 * b + c
                piece = t[64 * c : 64 * c + 32] + t[64 * c + 32 : 64 * c + 64]
                send[l, k % 2, k // 2] = send[l, k % 2, k // 2] + piece

    near = [(min(i, 4 - i) + min(j, 4 - j), i, j) for i in range(4) for j in range(4)]
    others = [(i, j) for d, i, j in sorted(near, reverse=True) if d > 0]

    def plane_index(l, hand, i, j):
        if l == 1:
            return (me.y + i) % 4 * 4 + (me.x + j) % 4
        return (me.y * (1 - hand) + me.x * hand + i) % 4 * 4 + (me.z + j) % 4

    def plane_peer(l, i, j):
        return me.at(i, j, 0) if l == 1 else me.at(i * one, i * core, j)

    def axis_index(l):
        return me.z if l == 1 else me.x * one + me.y * core

    def axis_peer(l, i):
        return me.at(0, 0, i) if l == 1 else me.at(i * core, i * one, 0)

    pending, forwards = [], {}

    def push(src, dst, sems, l, n, peer):
        copy = pltpu.make_async_remote_copy(
            src_ref=src, dst_ref=dst, send_sem=sems[0].at[l, n], recv_sem=sems[1].at[l, n],
            device_id=peer, device_id_type=MESH,
        )
        copy.start()
        pending.append(copy)
        return copy

    ar_sems = (ar_send, ar_recv)
    pair_sems = (pair_send, pair_recv)
    bounds = (((0, 4), (4, 9), (9, 14)), ((0, 5), (5, 9), (9, 14)))

    def pair_step(l, n):
        low, high = bounds[l][n]
        part = pl.ds(low, high - low)
        return push(
            send.at[l, one, part], r0.at[l, part], pair_sems, l, n, me.at(0, 0, 0, 1)
        )

    def pair_add(l, n, copy):
        copy.wait_recv()
        for t in range(*bounds[l][n]):
            send[l, core, t] = send[l, core, t] + r0[l, t]

    def all_reduce(l):
        here = plane_index(l, core, 0, 0)
        copies = [
            push(
                send.at[l, core, plane_index(l, core, i, j)], r1.at[l, n],
                ar_sems, l, n, plane_peer(l, i, j),
            )
            for n, (i, j) in enumerate(others)
        ]
        yield
        total = send[l, core, here]
        for n in range(14, -1, -1):
            copies[n].wait_recv()
            total = total + r1[l, n]
        i3 = axis_index(l)
        r2[l, i3] = total
        copies = [
            push(r2.at[l, i3], r2.at[l, i3], ar_sems, l, 14 + i, axis_peer(l, i))
            for i in range(1, 4)
        ]
        yield
        for copy in copies:
            copy.wait_recv()
        fin[l, core, here] = (r2[l, 0] + r2[l, 1]) + (r2[l, 2] + r2[l, 3])
        copies = [
            push(
                fin.at[l, core, here], fin.at[l, core, here], ar_sems, l, 18 + n,
                plane_peer(l, i, j),
            )
            for n, (i, j) in enumerate(others)
        ]
        forward(l, 0, 0, 0)
        yield copies

    def forward(l, n, i, j):
        slot = fin.at[l, core, plane_index(l, core, i, j)]
        forwards[l, n] = push(slot, slot, ar_sems, l, 33 + n, me.at(0, 0, 0, 1))

    def right_tap(l, hand, i, j, sums):
        mat = mat_first if l == 0 else mat_second
        tap = plane_index(l, hand, i, j)
        k = 2 * tap + hand
        row = pl.multiple_of(jnp.minimum(k, 26) * 256, 256)
        mh, ml = split(mat[pl.ds(row, 256), :])
        both = jnp.concatenate(split(fin[l, hand, tap]), 0)
        flat[l, k] = both
        t = mm(both, mh)
        return sums + (t[:RANK] + (t[RANK:] + mm(both[:RANK], ml)))

    def gram_table(l):
        gram = jnp.zeros((2 * RANK, 2 * RANK), F32)
        for k in range(27):
            gram = gram + mm(flat[l, k], flat[l, k], NT)
        gram = (gram[:RANK, :RANK] + gram[RANK:, RANK:]) + (
            gram[:RANK, RANK:] + gram[RANK:, :RANK]
        )
        return jnp.concatenate([gram, eye], 1)

    def right_terms(l, copies, middle=lambda: None):
        sums = jnp.zeros((RANK, C), F32)
        done = [(0, 0)]
        for low, high in ((7, 15), (0, 7)):
            for n in range(high - 1, low - 1, -1):
                sender = others[n]
                source = (-sender[0]) % 4, (-sender[1]) % 4
                copies[n].wait_recv()
                forward(l, 1 + n, *source)
                done.append(source)
            for i, j in done:
                sums = right_tap(l, core, i, j, sums)
            done = []
        rest = [(0, 0)] + [((-i) % 4, (-j) % 4) for i, j in others]
        for n in [0] + list(range(15, 0, -1)):
            forwards[l, n].wait_recv()
        middle()
        for n in [0] + list(range(15, 0, -1)):
            sums = right_tap(l, one, *rest[n], sums)
        srcv[l] = sums

    def right_reduce(l):
        s_sems = (s_send, s_recv)
        mine = srcv[l]
        for n, (index, step) in enumerate(((me.y, (1, 0, 0)), (me.x, (0, 1, 0)))):
            slot = 4 * n + index
            sall[l, slot] = mine
            copies = [
                push(
                    sall.at[l, slot], sall.at[l, slot], s_sems, l, 3 * n + i - 1,
                    me.at(*(i * v for v in step)),
                )
                for i in range(1, 4)
            ]
            yield
            for copy in copies:
                copy.wait_recv()
            mine = (sall[l, 4 * n] + sall[l, 4 * n + 1]) + (sall[l, 4 * n + 2] + sall[l, 4 * n + 3])
        slot = 8 + 2 * me.z + core
        sall[l, slot] = mine
        copies = [
            push(sall.at[l, slot], sall.at[l, slot], s_sems, l, 5 + i, me.at(0, 0, i // 2, i % 2))
            for i in range(1, 8)
        ]
        yield
        for copy in copies:
            copy.wait_recv()
        total = [sall[l, 8 + 2 * i] + sall[l, 9 + 2 * i] for i in range(4)]
        right_out[l] = precise(tables[l][:, RANK:], (total[0] + total[1]) + (total[2] + total[3]))
        yield

    def grad_step(l, planes, source, first, i):
        b, c = i // 3, i % 3
        r = (2 - b) * WW
        right = source[c, first : first + 2, r : r + CELLS, :].reshape(2 * CELLS, C)
        for a in range(3):
            rows = slice((9 * a + i) * 256, (9 * a + i + 1) * 256)
            g = mm(planes[a : a + 2].reshape(2 * CELLS, C), right, TN)
            mat = mat_first if l == 0 else mat_second
            mat[rows, :] = g + err[l, rows, :].astype(F32)

    def back_part(d, a):
        x = jnp.concatenate(
            [
                cv[c, d + 2 - a, (2 - b) * WW : (2 - b) * WW + CELLS, :]
                for b in range(3)
                for c in range(3)
            ],
            1,
        )
        w = jnp.concatenate([ker[9 * a + i] for i in range(9)], 1)
        return mm(x, w, NT)

    loads[0].wait()
    for plane in (1, 2):
        right_factor(1, bq_second, plane, cot[plane])
    loads[1].wait()
    for plane in (1, 2):
        act[plane] = jnp.maximum(act[plane], jnp.zeros((CELLS, C), BF))
    loads[2].wait()
    error_left(1)
    grad_left(1, 1, bq_second[1:3], act[1:3])
    pl.semaphore_wait(barrier, len(peers))
    send_halos()
    pairs = {1: pair_step(1, 1)}
    grad_left(1, 0, bq_second[2:3], act[1:2])
    grad_left(1, 2, bq_second[1:2], act[2:3])
    for plane in (1, 2):
        store_shifts(cv, plane, cot[plane])
    loads[3].wait()
    acc[0] = back_part(0, 0) + back_part(0, 1)
    acc[1] = back_part(1, 1) + back_part(1, 2)
    pair_add(1, 1, pairs[1])
    loads[4].wait()
    error_left(0)
    wait_halo(0)
    for plane in (0, 3):
        right_factor(1, bq_second, plane, masked(cot, plane))
    grad_left(1, 0, bq_second[3:4], act[2:3])
    pairs[0] = pair_step(1, 0)
    grad_left(1, 2, bq_second[0:1], act[1:2])
    pairs[2] = pair_step(1, 2)
    for plane in (0, 3):
        store_shifts(cv, plane, masked(cot, plane))
    total = acc[0] + back_part(0, 2)
    gate[0] = jnp.where(act[1] > 0, total, 0.0).astype(BF)
    pair_add(1, 0, pairs[0])
    pair_add(1, 2, pairs[2])
    second = all_reduce(1)
    next(second)
    total = acc[1] + back_part(1, 0)
    gate[1] = jnp.where(act[2] > 0, total, 0.0).astype(BF)
    for d in range(2):
        right_factor(0, bq_first, d, gate[d])
    loads[5].wait()
    wait_halo(1)
    for plane in (0, 3):
        vol[plane] = masked(vol, plane)
    pairs = []
    for a in range(3):
        grad_left(0, a, bq_first[...], vol[a : a + 2])
        pairs.append(pair_step(0, a))
        if a > 0:
            pair_add(0, a - 1, pairs[a - 1])
    for d in range(2):
        store_shifts(gv, d, gate[d])
    wait_halo(2)
    for plane in (0, 3):
        act[plane] = jnp.maximum(masked(act, plane), jnp.zeros((CELLS, C), BF))
    pair_add(0, 2, pairs[2])
    first = all_reduce(0)
    next(first)
    grad_step(1, act, cv, 1, 0)
    grad_step(1, act, cv, 1, 1)
    next(second)
    for i in range(2, 8):
        grad_step(1, act, cv, 1, i)
    next(first)
    second_copies = next(second)
    grad_step(1, act, cv, 1, 8)
    for i in range(0, 4):
        grad_step(0, vol, gv, 0, i)
    first_copies = next(first)
    for i in range(4, 9):
        grad_step(0, vol, gv, 0, i)

    eye = (
        lax.broadcasted_iota(jnp.int32, (RANK, RANK), 0)
        == lax.broadcasted_iota(jnp.int32, (RANK, RANK), 1)
    ).astype(F32)
    rows = lax.broadcasted_iota(jnp.int32, (RANK, 2 * RANK), 0)
    tables = [None, None]

    def eliminate(l, j0, j1):
        t = tables[l]
        for j in range(j0, j1):
            row = t[j : j + 1, :] * (1.0 / t[j : j + 1, j : j + 1])
            t = jnp.where(rows == j, row, t - t[:, j : j + 1] * row)
        tables[l] = t

    right_terms(1, second_copies)
    sum_second = right_reduce(1)
    next(sum_second)
    tables[1] = gram_table(1)
    eliminate(1, 0, 4)
    right_terms(0, first_copies, lambda: eliminate(1, 4, 14))
    sum_first = right_reduce(0)
    next(sum_first)
    next(sum_second)
    tables[0] = gram_table(0)
    eliminate(1, 14, 24)
    eliminate(0, 0, 10)
    next(sum_second)
    next(sum_first)
    eliminate(1, 24, 32)
    eliminate(0, 10, 23)
    next(sum_first)
    eliminate(0, 23, 32)
    next(sum_second)
    right = stacked_right(right_out[1])
    for k in range(27):
        part = slice(k * 256, (k + 1) * 256)
        tail[part, :] = (mat_second[part, :] - left_product(flat[1, k], right)).astype(BF)
    next(sum_first)
    for copy in pending:
        copy.wait_send()


def last_kernel(
    start_ref, mat_ref, left_ref, right_ref, tail_ref, err_hbm, sum_out, done, span, sems
):
    copies = [pltpu.make_async_copy(tail_ref, err_hbm.at[1], sems.at[0])]
    copies[0].start()
    right = stacked_right(right_ref[0])
    for i in range(9):
        for k in range(3 * i, 3 * i + 3):
            part = slice(k * 256, (k + 1) * 256)
            done[part, :] = (mat_ref[part, :] - left_product(left_ref[0, k], right)).astype(BF)
        part = pl.ds(768 * i, 768)
        copies.append(pltpu.make_async_copy(done.at[part], err_hbm.at[0, part], sems.at[1 + i]))
        copies[-1].start()
    start = start_ref[0]
    k = jnp.minimum(start // 256, 25)
    for l in range(2):
        right = stacked_right(right_ref[l])
        for j in range(2):
            span[l, 256 * j : 256 * (j + 1), :] = left_product(left_ref[l, k + j], right) * 128.0
        sum_out[l] = span[l, pl.ds(pl.multiple_of(start - k * 256, 8), ROWS // 32), :]
    for copy in copies:
        copy.wait()


def per_device(volume, pre_act, cotangent, kernel_second, q_start, error):
    def rows(x):
        return x.reshape(2, CELLS, C)

    hbm = pl.BlockSpec(memory_space=pltpu.HBM)
    vmem = pl.BlockSpec(memory_space=pltpu.VMEM)
    dma = pltpu.SemaphoreType.DMA
    V = pltpu.VMEM
    mat, left, right, tail = pl.pallas_call(
        main_kernel,
        out_shape=(
            V((ROWS, C), F32), V((2, 32, 2 * RANK, C), BF), V((2, RANK, C), F32), V((ROWS, C), BF),
        ),
        in_specs=[hbm] * 5 + [vmem],
        out_specs=(vmem, vmem, vmem, vmem),
        scratch_shapes=[
            V((4, CELLS, C), BF), V((4, CELLS, C), BF), V((4, CELLS, C), BF),
            V((27, C, C), BF), V((2, ROWS, C), BF), V((3, 4, PAD, C), BF), V((3, 2, PAD, C), BF),
            V((2, PAD, 6 * RANK), BF), V((4, PAD, 6 * RANK), BF),
            V((2, CELLS, C), F32), V((2, CELLS, C), BF), V((ROWS, C), F32),
            V((2, 2, 16, RANK, C), F32), V((2, 14, RANK, C), F32), V((2, 15, RANK, C), F32),
            V((2, 4, RANK, C), F32), V((2, 2, 16, RANK, C), F32),
            V((2, RANK, C), F32), V((2, 16, RANK, C), F32),
            dma((6,)), dma((3, 2)), dma((3, 2)), dma((2, 3)), dma((2, 3)), dma((2, 49)),
            dma((2, 49)), dma((2, 13)), dma((2, 13)),
        ],
        compiler_params=pltpu.CompilerParams(
            collective_id=0, has_side_effects=True, vmem_limit_bytes=MAIN_VMEM << 20
        ),
        name="main_kernel",
    )(
        rows(pre_act), rows(cotangent), rows(volume), kernel_second,
        error.reshape(2, ROWS, C), jnp.swapaxes(q_start, 1, 2),
    )
    start = (lax.axis_index("slab") * (ROWS // 32)).astype(jnp.int32).reshape(1)
    new_error, summed = pl.pallas_call(
        last_kernel,
        out_shape=(
            jax.ShapeDtypeStruct((2, ROWS, C), BF),
            jax.ShapeDtypeStruct((2, ROWS // 32, C), F32),
        ),
        in_specs=[pl.BlockSpec(memory_space=pltpu.SMEM), vmem, vmem, vmem, vmem],
        out_specs=(hbm, vmem),
        scratch_shapes=[V((ROWS, C), BF), V((2, 512, C), F32), dma((10,))],
        compiler_params=pltpu.CompilerParams(vmem_limit_bytes=LAST_VMEM << 20),
        name="last_kernel",
    )(start, mat, left, right, tail)
    return (summed, new_error.reshape(1, 1, 2, ROWS, C))


def solution(mesh):
    in_specs = (
        P("dp", "slab", None, None, None),
        P("dp", "slab", None, None, None),
        P("dp", "slab", None, None, None),
        P(),
        P(),
        P("dp", "slab", None, None, None),
    )
    out_specs = (P(None, "slab", None), P("dp", "slab", None, None, None))
    return jax.shard_map(
        per_device, mesh=mesh, in_specs=in_specs, out_specs=out_specs, check_vma=False
    )
```

time: 80.5 us -> 73.8 us (0.917)
  Pallas kernels: 79.7 us -> 72.8 us
    pallas_call x2, Pallas kernels: 79.7 us -> 72.8 us  [the longest x1 69 us: per_device(): pl.pallas_call(main_kernel, out_shape=(V((ROWS, C), F32), V((2, 32, 2 * R...]
where the time goes in v3:
time: 73.8 us; the launch traced here: 73.6 us
  Pallas kernels  72.8 us (99%)
  between operations  0.82 us (1%)
    pallas_call x1, Pallas kernels, per_device(): pl.pallas_call(main_kernel, out_shape=(V((ROWS, C), F32), V((2, 32, 2 * R...  69 us
    pallas_call x1, Pallas kernels, per_device(): pl.pallas_call(last_kernel, out_shape=(jax.ShapeDtypeStruct((2, ROWS, C),...  3.75 us

profile of v3, /device:TPU:1, one launch (start us, length us, event | category | flops | bytes accessed | tf_op | source)
XLA Modules:
  0.0 73.6 jit_solution(8740432633301306280)
XLA Ops:
  0.6 69.0 %main_kernel.1 = (f32[6912,256]{1,0:T(8,128)S(1)}, bf16[2,32,64,256]{3,2,1,0:T(8,128)(2,1)S(1)}, f32[2,32,256]{2,1,0:T(8,128)S(1)}, bf16[6912,256]{1,0:T(8,128)(2,1)S(1)}) custom-call(bf16[2,512,256]{2,1,0:T(8,128)(2,1)} %bitcast.8, bf16[2,512,256]{2,1,0:T(8,128)(2,1)} %bitcast.9, bf16[2,512,256]{2,1,0:T(8,128)(2,1)} %bitcast.10, ...), custom_call_target="tpu_custom_call" | custom-call | tf_op jit(solution)/shard_map/main_kernel/pallas_call | solution.py:489
  69.7 3.8 %last_kernel.1 = (bf16[2,6912,256]{2,1,0:T(8,128)(2,1)}, f32[2,216,256]{2,1,0:T(8,128)}) custom-call(s32[1]{0:T(128)} %bitcast.start_ref, f32[6912,256]{1,0:T(8,128)S(1)} %get-tuple-element.8.mat_ref, bf16[2,32,64,256]{3,2,1,0:T(8,128)(2,1)S(1)} %get-tuple-element.9.left_ref, f32[2,32,256]{2,1,0:T(8,128)S(1)} %get-tuple-element.10.right_ref, ...), custom_call_target="tpu_custom_call" | custom-call | tf_op jit(solution)/shard_map/last_kernel/pallas_call | solution.py:516

commit v4 on v3

--- a/solution.py
+++ b/solution.py
@@ -142,6 +142,14 @@
         for k in range(27, 32):
             send[l, k % 2, k // 2] = jnp.zeros((RANK, C), F32)
 
+    def error_half(l, hand, add):
+        for t in range(14):
+            k = 2 * t + hand
+            row = pl.multiple_of(jnp.minimum(k, 26) * 256, 256)
+            value = mm(q2[l], err[l, pl.ds(row, 256), :], NT)
+            value = jnp.where(k < 27, value[:RANK] + value[RANK:], 0.0)
+            send[l, hand, t] = send[l, hand, t] + value if add else value
+
     def right_factor(l, dst, d, x):
         t = mm(x, q2[l], NT)
         t = t[:, :RANK] + t[:, RANK:]
@@ -195,6 +203,11 @@
     ar_sems = (ar_send, ar_recv)
     pair_sems = (pair_send, pair_recv)
     bounds = (((0, 4), (4, 9), (9, 14)), ((0, 5), (5, 9), (9, 14)))
+
+    def settle():
+        for copy in pending:
+            copy.wait_send()
+        pending.clear()
 
     def pair_step(l, n):
         low, high = bounds[l][n]
@@ -246,9 +259,8 @@
         slot = fin.at[l, core, plane_index(l, core, i, j)]
         forwards[l, n] = push(slot, slot, ar_sems, l, 33 + n, me.at(0, 0, 0, 1))
 
-    def right_tap(l, hand, i, j, sums):
+    def right_tap(l, hand, tap, sums):
         mat = mat_first if l == 0 else mat_second
-        tap = plane_index(l, hand, i, j)
         k = 2 * tap + hand
         row = pl.multiple_of(jnp.minimum(k, 26) * 256, 256)
         mh, ml = split(mat[pl.ds(row, 256), :])
@@ -277,14 +289,13 @@
                 forward(l, 1 + n, *source)
                 done.append(source)
             for i, j in done:
-                sums = right_tap(l, core, i, j, sums)
+                sums = right_tap(l, core, plane_index(l, core, i, j), sums)
             done = []
-        rest = [(0, 0)] + [((-i) % 4, (-j) % 4) for i, j in others]
         for n in [0] + list(range(15, 0, -1)):
             forwards[l, n].wait_recv()
         middle()
-        for n in [0] + list(range(15, 0, -1)):
-            sums = right_tap(l, one, *rest[n], sums)
+        for t in range(14):
+            sums = right_tap(l, one, t, sums)
         srcv[l] = sums
 
     def right_reduce(l):
@@ -360,7 +371,9 @@
     acc[1] = back_part(1, 1) + back_part(1, 2)
     pair_add(1, 1, pairs[1])
     loads[4].wait()
-    error_left(0)
+    error_half(0, one, False)
+    for t in range(16):
+        send[0, core, t] = jnp.zeros((RANK, C), F32)
     wait_halo(0)
     for plane in (0, 3):
         right_factor(1, bq_second, plane, masked(cot, plane))
@@ -390,14 +403,15 @@
         pairs.append(pair_step(0, a))
         if a > 0:
             pair_add(0, a - 1, pairs[a - 1])
+    error_half(0, core, True)
+    pair_add(0, 2, pairs[2])
+    first = all_reduce(0)
+    next(first)
     for d in range(2):
         store_shifts(gv, d, gate[d])
     wait_halo(2)
     for plane in (0, 3):
         act[plane] = jnp.maximum(masked(act, plane), jnp.zeros((CELLS, C), BF))
-    pair_add(0, 2, pairs[2])
-    first = all_reduce(0)
-    next(first)
     grad_step(1, act, cv, 1, 0)
     grad_step(1, act, cv, 1, 1)
     next(second)
@@ -442,6 +456,7 @@
     next(sum_first)
     eliminate(1, 24, 32)
     eliminate(0, 10, 23)
+    settle()
     next(sum_first)
     eliminate(0, 23, 32)
     next(sum_second)
@@ -450,30 +465,31 @@
         part = slice(k * 256, (k + 1) * 256)
         tail[part, :] = (mat_second[part, :] - left_product(flat[1, k], right)).astype(BF)
     next(sum_first)
-    for copy in pending:
-        copy.wait_send()
+    settle()
 
 
 def last_kernel(
-    start_ref, mat_ref, left_ref, right_ref, tail_ref, err_hbm, sum_out, done, span, sems
+    start_ref, mat_ref, left_ref, right_ref, tail_ref, err_hbm, sum_hbm, done, span, sems
 ):
     copies = [pltpu.make_async_copy(tail_ref, err_hbm.at[1], sems.at[0])]
     copies[0].start()
+    start = start_ref[0]
+    k = jnp.minimum(start // 256, 25)
+    part = pl.ds(pl.multiple_of(start - k * 256, 8), ROWS // 32)
+    for l in range(2):
+        right = stacked_right(right_ref[l])
+        for j in range(2):
+            span[l, 256 * j : 256 * (j + 1), :] = left_product(left_ref[l, k + j], right) * 128.0
+        copies.append(pltpu.make_async_copy(span.at[l, part], sum_hbm.at[l], sems.at[1 + l]))
+        copies[-1].start()
     right = stacked_right(right_ref[0])
     for i in range(9):
         for k in range(3 * i, 3 * i + 3):
             part = slice(k * 256, (k + 1) * 256)
             done[part, :] = (mat_ref[part, :] - left_product(left_ref[0, k], right)).astype(BF)
         part = pl.ds(768 * i, 768)
-        copies.append(pltpu.make_async_copy(done.at[part], err_hbm.at[0, part], sems.at[1 + i]))
+        copies.append(pltpu.make_async_copy(done.at[part], err_hbm.at[0, part], sems.at[3 + i]))
         copies[-1].start()
-    start = start_ref[0]
-    k = jnp.minimum(start // 256, 25)
-    for l in range(2):
-        right = stacked_right(right_ref[l])
-        for j in range(2):
-            span[l, 256 * j : 256 * (j + 1), :] = left_product(left_ref[l, k + j], right) * 128.0
-        sum_out[l] = span[l, pl.ds(pl.multiple_of(start - k * 256, 8), ROWS // 32), :]
     for copy in copies:
         copy.wait()
 
@@ -520,8 +536,8 @@
             jax.ShapeDtypeStruct((2, ROWS // 32, C), F32),
         ),
         in_specs=[pl.BlockSpec(memory_space=pltpu.SMEM), vmem, vmem, vmem, vmem],
-        out_specs=(hbm, vmem),
-        scratch_shapes=[V((ROWS, C), BF), V((2, 512, C), F32), dma((10,))],
+        out_specs=(hbm, hbm),
+        scratch_shapes=[V((ROWS, C), BF), V((2, 512, C), F32), dma((12,))],
         compiler_params=pltpu.CompilerParams(vmem_limit_bytes=LAST_VMEM << 20),
         name="last_kernel",
     )(start, mat, left, right, tail)

time: 73.8 us -> 72 us (0.976)
  Pallas kernels: 72.8 us -> 71 us
    pallas_call x1, Pallas kernels: 69 us -> 67.8 us  [per_device(): pl.pallas_call(main_kernel, out_shape=(V((ROWS, C), F32), V((2, 32, 2 * R...]
where the time goes in v4:
time: 72 us; the launch traced here: 71.8 us
  Pallas kernels  71 us (99%)
  between operations  0.82 us (1%)
    pallas_call x1, Pallas kernels, per_device(): pl.pallas_call(main_kernel, out_shape=(V((ROWS, C), F32), V((2, 32, 2 * R...  67.8 us
    pallas_call x1, Pallas kernels, per_device(): pl.pallas_call(last_kernel, out_shape=(jax.ShapeDtypeStruct((2, ROWS, C),...  3.17 us

profile of v4, /device:TPU:1, one launch (start us, length us, event | category | flops | bytes accessed | tf_op | source)
XLA Modules:
  0.0 71.8 jit_solution(17634952221045197960)
XLA Ops:
  0.6 67.8 %main_kernel.1 = (f32[6912,256]{1,0:T(8,128)S(1)}, bf16[2,32,64,256]{3,2,1,0:T(8,128)(2,1)S(1)}, f32[2,32,256]{2,1,0:T(8,128)S(1)}, bf16[6912,256]{1,0:T(8,128)(2,1)S(1)}) custom-call(bf16[2,512,256]{2,1,0:T(8,128)(2,1)} %bitcast.8, bf16[2,512,256]{2,1,0:T(8,128)(2,1)} %bitcast.9, bf16[2,512,256]{2,1,0:T(8,128)(2,1)} %bitcast.10, ...), custom_call_target="tpu_custom_call" | custom-call | tf_op jit(solution)/shard_map/main_kernel/pallas_call | solution.py:505
  68.5 3.2 %last_kernel.1 = (bf16[2,6912,256]{2,1,0:T(8,128)(2,1)}, f32[2,216,256]{2,1,0:T(8,128)}) custom-call(s32[1]{0:T(128)} %bitcast.start_ref, f32[6912,256]{1,0:T(8,128)S(1)} %get-tuple-element.8.mat_ref, bf16[2,32,64,256]{3,2,1,0:T(8,128)(2,1)S(1)} %get-tuple-element.9.left_ref, f32[2,32,256]{2,1,0:T(8,128)S(1)} %get-tuple-element.10.right_ref, ...), custom_call_target="tpu_custom_call" | custom-call | tf_op jit(solution)/shard_map/last_kernel/pallas_call | solution.py:532

commit v5 on v4

--- a/solution.py
+++ b/solution.py
@@ -30,6 +30,13 @@
     xh, xl = split(x)
     yh, yl = split(y)
     return mm(xh, yh, dims) + (mm(xh, yl, dims) + mm(xl, yh, dims))
+
+
+def store_center(dst, plane, x):
+    zero = jnp.zeros((WW, C), BF)
+    dst[1, plane, 0:WW, :] = zero
+    dst[1, plane, WW : WW + CELLS, :] = x
+    dst[1, plane, WW + CELLS : PAD, :] = zero
 
 
 def store_shifts(dst, plane, x):
@@ -338,17 +345,19 @@
             mat = mat_first if l == 0 else mat_second
             mat[rows, :] = g + err[l, rows, :].astype(F32)
 
-    def back_part(d, a):
+    def back_part(d, a, c):
         x = jnp.concatenate(
-            [
-                cv[c, d + 2 - a, (2 - b) * WW : (2 - b) * WW + CELLS, :]
-                for b in range(3)
-                for c in range(3)
-            ],
-            1,
+            [cv[1, d + 2 - a, (2 - b) * WW : (2 - b) * WW + CELLS, :] for b in range(3)], 1
         )
-        w = jnp.concatenate([ker[9 * a + i] for i in range(9)], 1)
-        return mm(x, w, NT)
+        return mm(x, jnp.concatenate([ker[9 * a + 3 * b + c] for b in range(3)], 1), NT)
+
+    def back_done(d):
+        parts = [acc[d, c] + back_part(d, 2 - 2 * d, c) for c in range(3)]
+        w = lax.broadcasted_iota(jnp.int32, (CELLS, C), 0) % WW
+        up = jnp.where(w == WW - 1, 0.0, pltpu.roll(parts[0], CELLS - 1, 0))
+        down = jnp.where(w == 0, 0.0, pltpu.roll(parts[2], 1, 0))
+        total = parts[1] + up + down
+        gate[d] = jnp.where(act[1 + d] > 0, total, 0.0).astype(BF)
 
     loads[0].wait()
     for plane in (1, 2):
@@ -365,10 +374,11 @@
     grad_left(1, 0, bq_second[2:3], act[1:2])
     grad_left(1, 2, bq_second[1:2], act[2:3])
     for plane in (1, 2):
-        store_shifts(cv, plane, cot[plane])
+        store_center(cv, plane, cot[plane])
     loads[3].wait()
-    acc[0] = back_part(0, 0) + back_part(0, 1)
-    acc[1] = back_part(1, 1) + back_part(1, 2)
+    for c in range(3):
+        acc[0, c] = back_part(0, 0, c) + back_part(0, 1, c)
+        acc[1, c] = back_part(1, 1, c) + back_part(1, 2, c)
     pair_add(1, 1, pairs[1])
     loads[4].wait()
     error_half(0, one, False)
@@ -382,15 +392,13 @@
     grad_left(1, 2, bq_second[0:1], act[1:2])
     pairs[2] = pair_step(1, 2)
     for plane in (0, 3):
-        store_shifts(cv, plane, masked(cot, plane))
-    total = acc[0] + back_part(0, 2)
-    gate[0] = jnp.where(act[1] > 0, total, 0.0).astype(BF)
+        store_center(cv, plane, masked(cot, plane))
+    back_done(0)
     pair_add(1, 0, pairs[0])
     pair_add(1, 2, pairs[2])
     second = all_reduce(1)
     next(second)
-    total = acc[1] + back_part(1, 0)
-    gate[1] = jnp.where(act[2] > 0, total, 0.0).astype(BF)
+    back_done(1)
     for d in range(2):
         right_factor(0, bq_first, d, gate[d])
     loads[5].wait()
@@ -409,6 +417,7 @@
     next(first)
     for d in range(2):
         store_shifts(gv, d, gate[d])
+        store_shifts(cv, 1 + d, cot[1 + d])
     wait_halo(2)
     for plane in (0, 3):
         act[plane] = jnp.maximum(masked(act, plane), jnp.zeros((CELLS, C), BF))
@@ -513,7 +522,7 @@
             V((4, CELLS, C), BF), V((4, CELLS, C), BF), V((4, CELLS, C), BF),
             V((27, C, C), BF), V((2, ROWS, C), BF), V((3, 4, PAD, C), BF), V((3, 2, PAD, C), BF),
             V((2, PAD, 6 * RANK), BF), V((4, PAD, 6 * RANK), BF),
-            V((2, CELLS, C), F32), V((2, CELLS, C), BF), V((ROWS, C), F32),
+            V((2, 3, CELLS, C), F32), V((2, CELLS, C), BF), V((ROWS, C), F32),
             V((2, 2, 16, RANK, C), F32), V((2, 14, RANK, C), F32), V((2, 15, RANK, C), F32),
             V((2, 4, RANK, C), F32), V((2, 2, 16, RANK, C), F32),
             V((2, RANK, C), F32), V((2, 16, RANK, C), F32),

time: 72 us -> 72 us (level)
  no operation moved by 1% of the time
where the time goes in v5:
time: 72 us; the launch traced here: 71.9 us
  Pallas kernels  71 us (99%)
  between operations  0.82 us (1%)
    pallas_call x1, Pallas kernels, per_device(): pl.pallas_call(main_kernel, out_shape=(V((ROWS, C), F32), V((2, 32, 2 * R...  67.9 us
    pallas_call x1, Pallas kernels, per_device(): pl.pallas_call(last_kernel, out_shape=(jax.ShapeDtypeStruct((2, ROWS, C),...  3.17 us

profile of v5, /device:TPU:1, one launch (start us, length us, event | category | flops | bytes accessed | tf_op | source)
XLA Modules:
  0.0 71.9 jit_solution(13855322746461718810)
XLA Ops:
  0.6 67.9 %main_kernel.1 = (f32[6912,256]{1,0:T(8,128)S(1)}, bf16[2,32,64,256]{3,2,1,0:T(8,128)(2,1)S(1)}, f32[2,32,256]{2,1,0:T(8,128)S(1)}, bf16[6912,256]{1,0:T(8,128)(2,1)S(1)}) custom-call(bf16[2,512,256]{2,1,0:T(8,128)(2,1)} %bitcast.8, bf16[2,512,256]{2,1,0:T(8,128)(2,1)} %bitcast.9, bf16[2,512,256]{2,1,0:T(8,128)(2,1)} %bitcast.10, ...), custom_call_target="tpu_custom_call" | custom-call | tf_op jit(solution)/shard_map/main_kernel/pallas_call | solution.py:514
  68.5 3.2 %last_kernel.1 = (bf16[2,6912,256]{2,1,0:T(8,128)(2,1)}, f32[2,216,256]{2,1,0:T(8,128)}) custom-call(s32[1]{0:T(128)} %bitcast.start_ref, f32[6912,256]{1,0:T(8,128)S(1)} %get-tuple-element.8.mat_ref, bf16[2,32,64,256]{3,2,1,0:T(8,128)(2,1)S(1)} %get-tuple-element.9.left_ref, f32[2,32,256]{2,1,0:T(8,128)S(1)} %get-tuple-element.10.right_ref, ...), custom_call_target="tpu_custom_call" | custom-call | tf_op jit(solution)/shard_map/last_kernel/pallas_call | solution.py:541

commit v6 on v5

--- a/solution.py
+++ b/solution.py
@@ -493,9 +493,9 @@
         copies[-1].start()
     right = stacked_right(right_ref[0])
     for i in range(9):
-        for k in range(3 * i, 3 * i + 3):
-            part = slice(k * 256, (k + 1) * 256)
-            done[part, :] = (mat_ref[part, :] - left_product(left_ref[0, k], right)).astype(BF)
+        both = jnp.concatenate([left_ref[0, k] for k in range(3 * i, 3 * i + 3)], 1)
+        part = slice(768 * i, 768 * (i + 1))
+        done[part, :] = (mat_ref[part, :] - left_product(both, right)).astype(BF)
         part = pl.ds(768 * i, 768)
         copies.append(pltpu.make_async_copy(done.at[part], err_hbm.at[0, part], sems.at[3 + i]))
         copies[-1].start()

time: 72 us -> 72 us (level)
  no operation moved by 1% of the time
where the time goes in v6:
time: 72 us; the launch traced here: 71.8 us
  Pallas kernels  71 us (99%)
  between operations  0.82 us (1%)
    pallas_call x1, Pallas kernels, per_device(): pl.pallas_call(main_kernel, out_shape=(V((ROWS, C), F32), V((2, 32, 2 * R...  67.9 us
    pallas_call x1, Pallas kernels, per_device(): pl.pallas_call(last_kernel, out_shape=(jax.ShapeDtypeStruct((2, ROWS, C),...  3.12 us

profile of v6, /device:TPU:1, one launch (start us, length us, event | category | flops | bytes accessed | tf_op | source)
XLA Modules:
  0.0 71.8 jit_solution(15364811604869187652)
XLA Ops:
  0.6 67.9 %main_kernel.1 = (f32[6912,256]{1,0:T(8,128)S(1)}, bf16[2,32,64,256]{3,2,1,0:T(8,128)(2,1)S(1)}, f32[2,32,256]{2,1,0:T(8,128)S(1)}, bf16[6912,256]{1,0:T(8,128)(2,1)S(1)}) custom-call(bf16[2,512,256]{2,1,0:T(8,128)(2,1)} %bitcast.8, bf16[2,512,256]{2,1,0:T(8,128)(2,1)} %bitcast.9, bf16[2,512,256]{2,1,0:T(8,128)(2,1)} %bitcast.10, ...), custom_call_target="tpu_custom_call" | custom-call | tf_op jit(solution)/shard_map/main_kernel/pallas_call | solution.py:514
  68.5 3.1 %last_kernel.1 = (bf16[2,6912,256]{2,1,0:T(8,128)(2,1)}, f32[2,216,256]{2,1,0:T(8,128)}) custom-call(s32[1]{0:T(128)} %bitcast.start_ref, f32[6912,256]{1,0:T(8,128)S(1)} %get-tuple-element.8.mat_ref, bf16[2,32,64,256]{3,2,1,0:T(8,128)(2,1)S(1)} %get-tuple-element.9.left_ref, f32[2,32,256]{2,1,0:T(8,128)S(1)} %get-tuple-element.10.right_ref, ...), custom_call_target="tpu_custom_call" | custom-call | tf_op jit(solution)/shard_map/last_kernel/pallas_call | solution.py:541
